TPU v7x, 32 devices: a whole 2x2x4 slice. The times are simulated.
32 devices in a mesh: section: 2 (over x), expert: 4 (over z), dp: 4 (over y, core).
Axes of the slice: x: 2, y: 2, z: 4, core: 2. Of those that a mesh axis runs over, the one named last changes fastest.
Arguments:
- frames: bfloat16 [4, 32, 48, 1280], P(None, ('expert', 'dp')), may hold values from -6 to 6
- norm_gain: float32 [2, 1280], P('section'), may hold values from 0.1 to 1.9
- router: bfloat16 [2, 1280, 4], P('section'), may hold values from -0.15625 to 0.15625
- w_in: bfloat16 [2, 4, 1280, 256], P('section', 'expert'), may hold values from -0.15625 to 0.15625
- w_out: bfloat16 [2, 4, 256, 1280], P('section', 'expert'), may hold values from -0.375 to 0.375
- routing: int32 [2, 4, 32, 48, 1], P('section', None, ('expert', 'dp')), may hold values from 0 to 3; in each aligned block of 96 rows (0 to 95, 96 to 191, ..., all dimensions but the last counted through in order) at most 27 rows name the same one
- head_gain: float32 [1280], replicated, may hold values from 0.1 to 1.9
- head_weight: bfloat16 [1280, 8000], P(None, 'expert'), may hold values from -6 to 6
- frame_lengths: int32 [4, 32], P(None, ('expert', 'dp')), may hold values from 24 to 48
- labels: int32 [4, 32, 12], P(None, ('expert', 'dp')), may hold values from 1 to 7999
- label_lengths: int32 [4, 32], P(None, ('expert', 'dp')), may hold values from 1 to 12
Outputs:
- losses: float32 [8, 16], P('section', ('expert', 'dp'))
- head_grad: bfloat16 [1280, 8000], P(None, 'expert')
Inputs may be any that keep to these rules, and one draw needn't show every extreme that they name: `routing`: in each layer and micro-batch, within the frames of one device (aligned blocks of 96 frames), no expert is named by more than 27 frames.
All inputs are finite; a program needn't handle non-finite values.
Results may differ from a plain program's by a relative error of at most 0.015.
Values may be sent and summed in bfloat16 or wider, within the bound.
No kernel may reach another device: no remote copies, remote signals or barrier semaphores. Data moves between devices by JAX's collectives and lax.ppermute only.
A program may use at most 64 MiB of HBM per device.

v0:
```python
import jax
import jax.numpy as jnp
import numpy as np
from jax import lax
from jax.experimental import pallas as pl
from jax.experimental.pallas import tpu as pltpu
from jax.sharding import Mesh, PartitionSpec as P

EPSILON = 1e-06
LOG_ZERO = -1e30
VMEM_LIMIT = 12 * 1024 * 1024
LARGE_LIMIT = 24 * 1024 * 1024
LANES = 128
COLS = 16
PEAK, TOTAL, WHOLE = COLS - 3, COLS - 2, COLS - 3
BLOCK_ROWS = 256
NT = (((1,), (1,)), ((), ()))
NN = (((1,), (0,)), ((), ()))


def round_up(value, unit):
    return -(-value // unit) * unit


def vmem_spec():
    return pl.BlockSpec(memory_space=pltpu.VMEM)


def smem_spec():
    return pl.BlockSpec(memory_space=pltpu.SMEM)


def call(kernel, out_shape, flops=0, limit=VMEM_LIMIT, **options):
    return pl.pallas_call(
        kernel,
        out_shape=out_shape,
        compiler_params=pltpu.CompilerParams(vmem_limit_bytes=limit),
        cost_estimate=pl.CostEstimate(flops=flops, bytes_accessed=0, transcendentals=0),
        **options,
    )


def bf16_rows(count, width):
    return jax.ShapeDtypeStruct((count, width), jnp.bfloat16)


def as_mask(values):
    return values.astype(jnp.float32).astype(jnp.bfloat16)


def split_rows(values, out_refs, spare=None, note=None):
    size, width = out_refs[0].shape
    for turn, out_ref in enumerate(out_refs):
        part = values[turn * size : (turn + 1) * size]
        if note is not None:
            row = lax.broadcasted_iota(jnp.int32, (size, width), 0)
            part = jnp.where(row == spare, note, part)
        out_ref[...] = part.astype(jnp.bfloat16)


def join_rows(refs):
    return jnp.concatenate([ref[...].astype(jnp.float32) for ref in refs], axis=0)


def rms_scale(values, gain):
    values = values.astype(jnp.float32)
    scale = lax.rsqrt(jnp.mean(values * values, axis=-1, keepdims=True) + EPSILON)
    return (values * scale * gain).astype(jnp.bfloat16)


def expert_column(ids, frame_count):
    pairs = ids.shape[0]
    square = jnp.concatenate(
        [ids.astype(jnp.float32), jnp.full((LANES - pairs, LANES), -1.0, jnp.float32)], axis=0
    )
    turned = jnp.transpose(square, (1, 0)).astype(jnp.int32)
    return jnp.concatenate([turned[:frame_count, p : p + 1] for p in range(pairs)], axis=0)


def placement(column, member, experts, capacity):
    count = column.shape[0]
    relative = column ^ member
    lane = lax.broadcasted_iota(jnp.int32, (count, LANES), 1)
    one_hot = (lane == relative).astype(jnp.float32)
    before = lax.broadcasted_iota(jnp.int32, (count, count), 1) <= lax.broadcasted_iota(
        jnp.int32, (count, count), 0
    )
    rank = lax.dot_general(
        as_mask(before), one_hot.astype(jnp.bfloat16), NN, preferred_element_type=jnp.float32
    )
    start = (lane * capacity - 1).astype(jnp.float32)
    slots = jnp.sum(one_hot * (rank + start), axis=1, keepdims=True).astype(jnp.int32)
    places = lax.broadcasted_iota(jnp.int32, (count, experts * capacity), 1)
    return (places == slots).astype(jnp.float32)


def scatter_rows(rows, ids, member, experts, capacity, frame_count, out_refs):
    count = rows.shape[0]
    chosen = placement(expert_column(ids, frame_count), member, experts, capacity)
    tall = round_up(count, LANES)
    if tall > count:
        chosen = jnp.concatenate(
            [chosen, jnp.zeros((tall - count, chosen.shape[1]), jnp.float32)], axis=0
        )
    pick = jnp.transpose(chosen, (1, 0))[:, :count].astype(jnp.bfloat16)
    placed = lax.dot_general(pick, rows, NN, preferred_element_type=jnp.float32)
    split_rows(placed, out_refs)


def combine_rows(rows, returned, ids, table, member, experts, capacity, frame_count):
    column = expert_column(ids, frame_count)
    pick = placement(column, member, experts, capacity).astype(jnp.bfloat16)
    normed = rms_scale(rows, table[:1])
    router = jnp.concatenate(
        [table[8:], jnp.zeros((LANES + 8 - table.shape[0], rows.shape[1]), jnp.float32)], axis=0
    ).astype(jnp.bfloat16)
    logits = lax.dot_general(normed, router, NT, preferred_element_type=jnp.float32)
    lane = lax.broadcasted_iota(jnp.int32, logits.shape, 1)
    gate = jax.nn.sigmoid(jnp.sum(jnp.where(lane == column, logits, 0.0), axis=1, keepdims=True))
    stacked = join_rows(returned).astype(jnp.bfloat16)
    mixed = lax.dot_general(pick, stacked, NN, preferred_element_type=jnp.float32)
    return (rows.astype(jnp.float32) + gate * mixed).astype(jnp.bfloat16)


def dispatch(rows, ids, member, experts, capacity, frame_count):
    width = rows.shape[1]

    def kernel(member_ref, rows_ref, ids_ref, *out_refs):
        scatter_rows(
            rows_ref[...], ids_ref[...], member_ref[0], experts, capacity, frame_count, out_refs
        )

    return call(
        kernel,
        tuple(bf16_rows(capacity, width) for _ in range(experts)),
        1 << 27,
        in_specs=[smem_spec()] + [vmem_spec()] * 2,
        out_specs=tuple(vmem_spec() for _ in range(experts)),
    )(member, rows, ids)


def pick_table(pick_ref, tables):
    if len(tables) == 1:
        return tables[0][...]
    return jnp.where(pick_ref[0] == 1, tables[0][...], tables[1][...])


def note_row(first_ref, labels_ref, frames_ref, counts_ref, pairs, width):
    utt_dev, label_max = labels_ref.shape[1:]
    lane = lax.broadcasted_iota(jnp.int32, (1, width), 1)
    row = jnp.zeros((1, width), jnp.int32)
    for pair in range(pairs):
        index = first_ref[0] + pair
        micro, utt = index // utt_dev, index % utt_dev
        values = [labels_ref[micro, utt, c] for c in range(label_max)]
        values += [frames_ref[utt, micro], counts_ref[utt, micro]]
        for c, value in enumerate(values):
            row = jnp.where(lane == pair * COLS + c, value // LANES, row)
            row = jnp.where(lane == LANES + pair * COLS + c, value % LANES, row)
    return row.astype(jnp.float32)


def run_expert(received, tables, own, other, pick_own, spare, note, pairs):
    count = len(received)
    capacity, width = received[0].shape
    others, choices = len(other), len(tables)
    noted = [] if note is None else list(note)

    def kernel(pick_ref, in_ref, out_weight_ref, *refs):
        table_refs, refs = refs[:choices], refs[choices:]
        other_refs, refs = refs[: 2 * others], refs[2 * others :]
        received_refs, refs = refs[:count], refs[count:]
        out_refs = refs[len(noted) :]

        def work(pieces):
            gain = pick_table(pick_ref, table_refs)[:1]
            normed = rms_scale(join_rows(received_refs), gain)
            total = None
            for weight_in, weight_out in pieces:
                hidden = lax.dot_general(
                    normed, weight_in[...], NN, preferred_element_type=jnp.float32
                )
                active = (hidden / (1.0 + jnp.exp(-hidden))).astype(jnp.bfloat16)
                part = lax.dot_general(
                    active, weight_out[...], NN, preferred_element_type=jnp.float32
                )
                total = part if total is None else total + part
            row = note_row(*refs[: len(noted)], pairs, width) if noted else None
            split_rows(total, out_refs, spare, row)

        if others == 0:
            work([(in_ref, out_weight_ref)])
            return

        @pl.when(pick_ref[0] == 1)
        def _():
            work([(in_ref, out_weight_ref)])

        @pl.when(pick_ref[0] != 1)
        def _():
            work([(other_refs[2 * i], other_refs[2 * i + 1]) for i in range(others)])

    flat = [weight for pair in other for weight in pair]
    return call(
        kernel,
        tuple(bf16_rows(capacity, width) for _ in range(count)),
        4 * count * capacity * width * own[0].shape[1],
        in_specs=[smem_spec()] + [vmem_spec()] * (2 + choices + 2 * others + count)
        + [smem_spec()] * len(noted),
        out_specs=tuple(vmem_spec() for _ in range(count)),
    )(pick_own, *own, *tables, *flat, *received, *noted)


def combine_and_dispatch(
    rows, returned, ids, tables, pick_own, next_ids, member, experts, capacity, frame_count
):
    width = rows.shape[1]
    choices = len(tables)

    def kernel(member_ref, pick_ref, rows_ref, ids_ref, next_ref, *refs):
        table_refs, refs = refs[:choices], refs[choices:]
        returned_refs, x_ref, out_refs = refs[:experts], refs[experts], refs[experts + 1 :]
        mixed = combine_rows(
            rows_ref[...],
            returned_refs,
            ids_ref[...],
            pick_table(pick_ref, table_refs),
            member_ref[0],
            experts,
            capacity,
            frame_count,
        )
        x_ref[...] = mixed
        scatter_rows(
            mixed, next_ref[...], member_ref[0], experts, capacity, frame_count, out_refs
        )

    shapes = (bf16_rows(*rows.shape),) + tuple(
        bf16_rows(capacity, width) for _ in range(experts)
    )
    result = call(
        kernel,
        shapes,
        1 << 28,
        in_specs=[smem_spec()] * 2 + [vmem_spec()] * (3 + choices + experts),
        out_specs=tuple(vmem_spec() for _ in shapes),
    )(member, pick_own, rows, ids, next_ids, *tables, *returned)
    return result[0], result[1:]


def combine_and_norm(
    rows, returned, ids, tables, pick_own, head_gain, member, experts, capacity, frame_count
):
    choices = len(tables)

    def kernel(member_ref, pick_ref, rows_ref, ids_ref, head_ref, *refs):
        table_refs, refs = refs[:choices], refs[choices:]
        final = combine_rows(
            rows_ref[...],
            refs[:experts],
            ids_ref[...],
            pick_table(pick_ref, table_refs),
            member_ref[0],
            experts,
            capacity,
            frame_count,
        )
        refs[experts][...] = rms_scale(final, head_ref[...])

    return call(
        kernel,
        bf16_rows(*rows.shape),
        1 << 28,
        in_specs=[smem_spec()] * 2 + [vmem_spec()] * (3 + choices + experts),
        out_specs=vmem_spec(),
    )(member, pick_own, rows, ids, head_gain, *tables, *returned)


def half_weights(core, weight_in, weight_out):
    width, hidden = weight_in.shape
    half = hidden // 2

    def kernel(core_ref, in_ref, out_ref, half_in, half_out, sems):
        start = pl.multiple_of(core_ref[0] * half, half)
        copies = (
            pltpu.make_async_copy(in_ref.at[:, pl.ds(start, half)], half_in, sems.at[0]),
            pltpu.make_async_copy(out_ref.at[pl.ds(start, half)], half_out, sems.at[1]),
        )
        for copy in copies:
            copy.start()
        for copy in copies:
            copy.wait()

    return call(
        kernel,
        (bf16_rows(width, half), bf16_rows(half, width)),
        1 << 20,
        in_specs=[smem_spec()] + [pl.BlockSpec(memory_space=pl.ANY)] * 2,
        out_specs=(vmem_spec(), vmem_spec()),
        scratch_shapes=[pltpu.SemaphoreType.DMA((2,))],
    )(core, weight_in, weight_out)


def block_list(shard):
    return [(i, min(BLOCK_ROWS, shard - i)) for i in range(0, shard, BLOCK_ROWS)]


def label_rows(weight, notes, member, groups, pairs, spare, label_max, line):
    shard, width = weight.shape
    sources = len(notes)
    utterances = sources * groups * pairs
    entries = utterances * COLS

    def kernel(member_ref, weight_ref, *refs):
        note_refs = refs[:sources]
        out_ref, places_ref, names_ref, turned_ref = refs[sources:]
        place = member_ref[0]
        found = []
        for ref in note_refs:
            row = ref[...].astype(jnp.float32)[spare : spare + 1]
            found.append((row[:, :LANES] * LANES + row[:, LANES : 2 * LANES]).astype(jnp.int32))
        if line:
            ends = (place == 0) | (place == 3)
            found = [
                found[0],
                found[1],
                jnp.where(ends, found[2], found[3]),
                jnp.where(ends, found[3], found[2]),
            ]
        names_ref[...] = jnp.zeros(names_ref.shape, jnp.int32)
        for slot in range(sources):
            for pair in range(groups * pairs):
                row = (pair // pairs * sources + slot) * pairs + pair % pairs
                names_ref[row : row + 1, :COLS] = found[slot][:, pair * COLS : (pair + 1) * COLS]
        lane = lax.broadcasted_iota(jnp.int32, (utterances, LANES), 1)
        named = jnp.where(lane < label_max, names_ref[...], jnp.where(lane == label_max, 0, -1))
        local = named - place * shard
        local = jnp.where((named >= 0) & (local >= 0) & (local < shard), local, -1)
        square = jnp.concatenate(
            [
                local.astype(jnp.float32),
                jnp.full((LANES - utterances, LANES), -1.0, jnp.float32),
            ],
            axis=0,
        )
        turned = jnp.transpose(square, (1, 0))
        for utterance in range(utterances):
            turned_ref[utterance * COLS : (utterance + 1) * COLS] = jnp.broadcast_to(
                turned[:COLS, utterance : utterance + 1], (COLS, LANES)
            )
        places = turned_ref[:, :1].astype(jnp.int32)
        places_ref[...] = jnp.transpose(turned_ref[...], (1, 0))[:1].astype(jnp.int32)
        total = jnp.zeros((entries, width), jnp.float32)
        for first, size in block_list(shard):
            entry = first + lax.broadcasted_iota(jnp.int32, (entries, size), 1)
            total = total + lax.dot_general(
                as_mask(entry == places),
                weight_ref[first : first + size],
                NN,
                preferred_element_type=jnp.float32,
            )
        out_ref[...] = total.astype(jnp.bfloat16)

    return call(
        kernel,
        (
            bf16_rows(entries, width),
            jax.ShapeDtypeStruct((1, entries), jnp.int32),
            jax.ShapeDtypeStruct((utterances, LANES), jnp.int32),
        ),
        2 * shard * entries * width,
        LARGE_LIMIT,
        in_specs=[smem_spec()] + [vmem_spec()] * (1 + sources),
        out_specs=tuple(vmem_spec() for _ in range(3)),
        scratch_shapes=[pltpu.VMEM((entries, LANES), jnp.float32)],
    )(member, weight, *notes)


def head_logits(
    fill, first_slot, count, pieces, member, weight, label_weight, frame_count, earlier=None
):
    given = len(pieces)
    span, width = pieces[0].shape
    row_count = count * span
    shard = weight.shape[0]
    height = round_up(shard, BLOCK_ROWS)
    entries = row_count // frame_count * COLS
    first_entry = first_slot * entries // count
    others = [] if earlier is None else [earlier]
    ahead = 0 if earlier is None else earlier.shape[0]

    def kernel(member_ref, weight_ref, label_ref, *refs):
        piece_refs = refs[:given]
        logits_ref, rows_ref, stats_ref = refs[given + len(others) :]

        def put(slot, piece_ref):
            rows_ref[slot * span : (slot + 1) * span] = piece_ref[...]

        def put_if(condition, slot, piece_ref):
            @pl.when(condition)
            def _():
                put(slot, piece_ref)

        fill(member_ref[0], piece_refs, put, put_if)
        peak = jnp.full((1, row_count), LOG_ZERO, jnp.float32)
        total = jnp.zeros((1, row_count), jnp.float32)
        for first, size in block_list(shard):
            logits = lax.dot_general(
                weight_ref[first : first + size],
                rows_ref[...],
                NT,
                preferred_element_type=jnp.float32,
            )
            logits_ref[first : first + size] = logits
            before = peak
            peak = jnp.maximum(before, jnp.max(logits, axis=0, keepdims=True))
            total = total * jnp.exp(before - peak) + jnp.sum(
                jnp.exp(logits - peak), axis=0, keepdims=True
            )
        if height > shard:
            logits_ref[shard:] = jnp.full((height - shard, row_count), LOG_ZERO, jnp.float32)
        crossed = lax.dot_general(
            label_ref[first_entry : first_entry + entries],
            rows_ref[...],
            NT,
            preferred_element_type=jnp.float32,
        )
        owner = lax.broadcasted_iota(jnp.int32, (COLS, row_count), 1) // frame_count
        picked = jnp.zeros((COLS, row_count), jnp.float32)
        for utterance in range(entries // COLS):
            part = crossed[utterance * COLS : (utterance + 1) * COLS]
            picked = picked + jnp.where(owner == utterance, part, 0.0)
        place = lax.broadcasted_iota(jnp.int32, (COLS, row_count), 0)
        stats = jnp.where(place == PEAK, peak, picked)
        stats = jnp.where(place == TOTAL, total, stats)
        for slot in range(ahead):
            stats_ref[slot] = refs[given][slot]
        for slot in range(count):
            stats_ref[ahead + slot] = stats[:, slot * span : (slot + 1) * span]

    return call(
        kernel,
        (
            jax.ShapeDtypeStruct((height, row_count), jnp.float32),
            bf16_rows(row_count, width),
            jax.ShapeDtypeStruct((ahead + count, COLS, span), jnp.float32),
        ),
        2 * height * row_count * width,
        LARGE_LIMIT,
        in_specs=[smem_spec()] + [vmem_spec()] * (2 + given + len(others)),
        out_specs=tuple(vmem_spec() for _ in range(3)),
    )(member, weight, label_weight, *pieces, *others)


def fill_line(place, piece_refs, put, put_if):
    own, beside, middle, outward, far, last = piece_refs
    ends = (place == 0) | (place == 3)
    inner = (place == 1) | (place == 2)
    put(0, own)
    put(1, beside)
    put_if(ends, 2, outward)
    put_if(ends, 3, last)
    put_if(inner, 2, middle)
    put_if(inner, 3, far)


def fill_all(place, piece_refs, put, put_if):
    for slot, piece_ref in enumerate(piece_refs):
        put(slot, piece_ref)


def log_add(first, second):
    peak = jnp.maximum(first, second)
    return peak + jnp.log(jnp.exp(first - peak) + jnp.exp(second - peak))


def log_add3(first, second, third):
    peak = jnp.maximum(jnp.maximum(first, second), third)
    return peak + jnp.log(
        jnp.exp(first - peak) + jnp.exp(second - peak) + jnp.exp(third - peak)
    )


def ctc_pass(stats, slots, notes, frame_count, label_max, parts, kept):
    calls, sources = len(stats), len(stats[0])
    each, _, span = stats[0][0].shape
    count = calls * each
    row_count = count * span
    utterances = notes.shape[0]
    entries = utterances * COLS
    tall = round_up(span, LANES)

    def kernel(slots_ref, notes_ref, *refs):
        (
            out_ref,
            high_ref,
            low_ref,
            loss_ref,
            turn_ref,
            emission_ref,
            emit_blank,
            emit_label,
            blank_fwd,
            label_fwd,
            blank_bwd,
            label_bwd,
            occupancy_ref,
        ) = refs[calls * sources :]
        place = lax.broadcasted_iota(jnp.int32, (COLS, span), 0)
        turn_ref[...] = jnp.zeros(turn_ref.shape, jnp.float32)
        for slot in range(count):
            found = []
            for k in range(sources):
                where = slots_ref[k * count + slot]
                part = refs[k][where % each]
                for other in range(1, calls):
                    later = refs[other * sources + k][where % each]
                    part = jnp.where(where >= other * each, later, part)
                found.append(part)
            joined = found[0]
            peak = found[0][PEAK : PEAK + 1]
            for other in found[1:]:
                joined = joined + other
                peak = jnp.maximum(peak, other[PEAK : PEAK + 1])
            total = jnp.zeros((1, span), jnp.float32)
            for other in found:
                total = total + other[TOTAL : TOTAL + 1] * jnp.exp(other[PEAK : PEAK + 1] - peak)
            log_total = peak + jnp.log(total)
            turn_ref[:COLS, :span] = jnp.where(place == TOTAL, log_total, joined - log_total)
            emission_ref[slot * span : (slot + 1) * span] = jnp.transpose(turn_ref[...], (1, 0))[
                :span
            ]

        lane = lax.broadcasted_iota(jnp.int32, (utterances, LANES), 1)
        is_label = lane < label_max
        is_blank = lane <= label_max
        names = jnp.where(is_label, notes_ref[...], 0)
        earlier = pltpu.roll(names, 1, 1)
        skip = is_label & (lane >= 1) & (names != 0) & (names != earlier)
        later = pltpu.roll(names, LANES - 1, 1)
        skip_next = (lane < label_max - 1) & (later != 0) & (later != names)
        frames = notes_ref[:, label_max : label_max + 1]
        counts = notes_ref[:, label_max + 1 : label_max + 2]
        ends_blank = jnp.where(lane == counts, 0.0, LOG_ZERO)
        ends_label = jnp.where(lane == counts - 1, 0.0, LOG_ZERO)

        def spread(step, carry):
            row = emission_ref[pl.ds(step, utterances, stride=frame_count), :]
            blank = jnp.sum(jnp.where(lane == label_max, row, 0.0), axis=1, keepdims=True)
            emit_blank[step] = jnp.where(is_blank, blank, LOG_ZERO)
            emit_label[step] = jnp.where(is_label, row, LOG_ZERO)
            return carry

        lax.fori_loop(0, frame_count, spread, 0, unroll=16)

        def advance(step, carry):
            fwd_blank, fwd_label, bwd_blank, bwd_label = carry
            moved = jnp.where(lane == 0, LOG_ZERO, pltpu.roll(fwd_label, 1, 1))
            new_blank = log_add(fwd_blank, moved) + emit_blank[step]
            new_label = (
                log_add3(fwd_label, fwd_blank, jnp.where(skip, moved, LOG_ZERO))
                + emit_label[step]
            )
            alive = step < frames
            fwd_blank = jnp.where(alive, new_blank, fwd_blank)
            fwd_label = jnp.where(alive, new_label, fwd_label)
            blank_fwd[step] = fwd_blank
            label_fwd[step] = fwd_label

            back = frame_count - 1 - step
            out_blank = bwd_blank + emit_blank[back + 1]
            out_label = bwd_label + emit_label[back + 1]
            next_blank = pltpu.roll(out_blank, LANES - 1, 1)
            next_label = jnp.where(skip_next, pltpu.roll(out_label, LANES - 1, 1), LOG_ZERO)
            ended = back >= frames - 1
            bwd_blank = jnp.where(ended, ends_blank, log_add(out_blank, out_label))
            bwd_label = jnp.where(
                ended, ends_label, log_add3(out_label, next_blank, next_label)
            )
            blank_bwd[back] = bwd_blank
            label_bwd[back] = bwd_label
            return (fwd_blank, fwd_label, bwd_blank, bwd_label)

        first_blank = jnp.where(lane == 0, emit_blank[0], LOG_ZERO)
        first_label = jnp.where(lane == 0, emit_label[0], LOG_ZERO)
        blank_fwd[0] = first_blank
        label_fwd[0] = first_label
        blank_bwd[frame_count - 1] = ends_blank
        label_bwd[frame_count - 1] = ends_label
        fwd_blank, fwd_label, _, _ = lax.fori_loop(
            1, frame_count, advance, (first_blank, first_label, ends_blank, ends_label), unroll=4
        )
        end_state = jnp.sum(jnp.where(lane == counts, fwd_blank, 0.0), axis=1, keepdims=True)
        near_state = jnp.sum(jnp.where(lane == counts - 1, fwd_label, 0.0), axis=1, keepdims=True)
        log_like = log_add(end_state, near_state)
        turned_losses = jnp.transpose(jnp.broadcast_to(-log_like, (utterances, LANES)), (1, 0))
        for part in range(parts):
            first = part * utterances // parts
            loss_ref[:, part * kept : (part + 1) * kept] = turned_losses[:1, first : first + kept]

        def occupy(step, carry):
            blank = jnp.exp(blank_fwd[step] + blank_bwd[step] - log_like)
            label = jnp.exp(label_fwd[step] + label_bwd[step] - log_like)
            blank = jnp.sum(jnp.where(is_blank, blank, 0.0), axis=1, keepdims=True)
            label = jnp.where(is_label, label, 0.0)
            whole = blank + jnp.sum(label, axis=1, keepdims=True)
            filled = jnp.where(lane == label_max, blank, label)
            filled = jnp.where(lane == WHOLE, whole, filled)
            filled = jnp.where(step < frames, -filled, 0.0)
            row = emission_ref[pl.ds(step, utterances, stride=frame_count), :]
            occupancy_ref[pl.ds(step, utterances, stride=frame_count), :] = jnp.where(
                lane == TOTAL, row, filled
            )
            return carry

        lax.fori_loop(0, frame_count, occupy, 0, unroll=16)
        turned = jnp.transpose(occupancy_ref[...], (1, 0))[:COLS]
        out_ref[...] = turned
        row_place = lax.broadcasted_iota(jnp.int32, (COLS, row_count), 0)
        owner = lax.broadcasted_iota(jnp.int32, (COLS, row_count), 1) // frame_count
        source = jnp.where(row_place < WHOLE, turned, 0.0)
        for utterance in range(utterances):
            part = jnp.where(owner == utterance, source, 0.0)
            high = part.astype(jnp.bfloat16)
            high_ref[utterance * COLS : (utterance + 1) * COLS] = high
            low_ref[utterance * COLS : (utterance + 1) * COLS] = (
                part - high.astype(jnp.float32)
            ).astype(jnp.bfloat16)

    held = pltpu.VMEM((frame_count, utterances, LANES), jnp.float32)
    table = pltpu.VMEM((row_count, LANES), jnp.float32)
    return call(
        kernel,
        (
            jax.ShapeDtypeStruct((COLS, row_count), jnp.float32),
            bf16_rows(entries, row_count),
            bf16_rows(entries, row_count),
            jax.ShapeDtypeStruct((1, parts * kept), jnp.float32),
        ),
        1 << 26,
        in_specs=[smem_spec()] + [vmem_spec()] * (1 + calls * sources),
        out_specs=tuple(vmem_spec() for _ in range(4)),
        scratch_shapes=[pltpu.VMEM((LANES, tall), jnp.float32), table]
        + [held] * 6
        + [table],
    )(slots, notes, *[value for group in stats for value in group])


def head_gradient(logits, rows, occupancy, high, low, places, order, outputs, each):
    count = len(logits)
    row_count, width = rows[0].shape
    entries = places.shape[1]
    blocks = outputs * each

    def kernel(order_ref, *refs):
        logits_refs, rows_refs = refs[:count], refs[count : 2 * count]
        occupancy_ref, high_ref, low_ref, places_ref = refs[2 * count : 2 * count + 4]
        out_refs = refs[2 * count + 4 :]
        for block in range(blocks):
            start = pl.multiple_of(order_ref[block] * BLOCK_ROWS, BLOCK_ROWS)
            entry = start + lax.broadcasted_iota(jnp.int32, (BLOCK_ROWS, entries), 0)
            select = as_mask(entry == places_ref[...])
            total = None
            for g in range(count):
                lanes = slice(g * row_count, (g + 1) * row_count)
                scattered = lax.dot_general(
                    select, high_ref[:, lanes], NN, preferred_element_type=jnp.float32
                ) + lax.dot_general(
                    select, low_ref[:, lanes], NN, preferred_element_type=jnp.float32
                )
                whole = occupancy_ref[WHOLE : WHOLE + 1, lanes]
                log_total = occupancy_ref[TOTAL : TOTAL + 1, lanes]
                values = logits_refs[g][pl.ds(start, BLOCK_ROWS), :]
                grad = (scattered - jnp.exp(values - log_total) * whole).astype(jnp.bfloat16)
                part = lax.dot_general(
                    grad, rows_refs[g][...], NN, preferred_element_type=jnp.float32
                )
                total = part if total is None else total + part
            out_refs[block // each][
                block % each * BLOCK_ROWS : (block % each + 1) * BLOCK_ROWS
            ] = total.astype(jnp.bfloat16)

    return call(
        kernel,
        tuple(bf16_rows(each * BLOCK_ROWS, width) for _ in range(outputs)),
        2 * blocks * BLOCK_ROWS * count * row_count * (width + 2 * entries),
        LARGE_LIMIT,
        in_specs=[smem_spec()] + [vmem_spec()] * (2 * count + 4),
        out_specs=tuple(vmem_spec() for _ in range(outputs)),
    )(order, *logits, *rows, occupancy, high, low, places)


def assemble(pieces, offsets, height, whole=None):
    count = len(pieces)
    part, width = pieces[0].shape
    short = height % part
    started = [] if whole is None else [whole]

    def kernel(offsets_ref, *refs):
        out_ref, sems = refs[count + len(started) :]

        def each(act):
            for index in range(count):
                offset = pl.multiple_of(offsets_ref[index], part)

                @pl.when(offset + part <= height)
                def _():
                    act(
                        pltpu.make_async_copy(
                            refs[index], out_ref.at[pl.ds(offset, part)], sems.at[index]
                        )
                    )

                if short:

                    @pl.when(offset + part > height)
                    def _():
                        act(
                            pltpu.make_async_copy(
                                refs[index].at[pl.ds(0, short)],
                                out_ref.at[pl.ds(height - short, short)],
                                sems.at[index],
                            )
                        )

        each(lambda copy: copy.start())
        each(lambda copy: copy.wait())

    anywhere = pl.BlockSpec(memory_space=pl.ANY)
    return call(
        kernel,
        bf16_rows(height, width),
        in_specs=[smem_spec()] + [vmem_spec()] * count + [anywhere] * len(started),
        out_specs=anywhere,
        scratch_shapes=[pltpu.SemaphoreType.DMA((count,))],
        input_output_aliases={} if whole is None else {1 + count: 0},
    )(offsets, *pieces, *started)


def swap(value, axis):
    return lax.ppermute(value, axis, [(0, 1), (1, 0)])


def crossed(value, axis, by):
    count = lax.axis_size(axis)
    return lax.ppermute(value, axis, [(i, i ^ by) for i in range(count)])


def after(value, *others):
    return lax.optimization_barrier((value,) + others)[0]


LINE_ORDER = np.array([[0, 1, 2, 3], [1, 0, 2, 3], [2, 3, 1, 0], [3, 2, 1, 0]])
MIDDLE = [(1, 2), (2, 1)]
OUTWARD = [(1, 0), (2, 3)]


def slot_orders(count):
    return LINE_ORDER if count == 4 else np.tile(np.arange(count), (count, 1))


def slot_tables(count, groups):
    orders = slot_orders(count)
    tables = np.zeros((count, count, count), np.int32)
    for member in range(count):
        for k in range(count):
            source = member ^ k
            for slot in range(count):
                tables[member, k, slot] = list(orders[source]).index(orders[member][slot])
    tables = np.concatenate([tables + g * count for g in range(groups)], axis=2)
    return tables.reshape(count, groups * count * count)


def wide(ref, start, size):
    return ref[pl.ds(start, size), :].astype(jnp.float32)


def sum_sent(own, came, places):
    height, width = own.shape
    part = height // 4

    def kernel(places_ref, own_ref, came_ref, *out_refs):
        section, outer = places_ref[0], places_ref[1]
        starts = (
            (1 - outer) * part,
            outer * part,
            (2 + 1 - section) * part,
            (2 + section) * part,
        )
        for start, out_ref in zip(starts, out_refs):
            start = pl.multiple_of(start, part)
            out_ref[...] = (wide(own_ref, start, part) + wide(came_ref, start, part)).astype(
                jnp.bfloat16
            )

    return call(
        kernel,
        tuple(bf16_rows(part, width) for _ in range(4)),
        1 << 20,
        in_specs=[smem_spec()] + [vmem_spec()] * 2,
        out_specs=tuple(vmem_spec() for _ in range(4)),
    )(places, own, came)


def sum_kept(own, came, arrived, places, keep):
    height, width = own.shape
    part = height // 4
    count = len(arrived) // 2

    def kernel(places_ref, own_ref, came_ref, *refs):
        section, outer = places_ref[0], places_ref[1]
        if not keep:
            section, outer = 1 - section, 1 - outer
        for side, start in enumerate((outer * part, (2 + section) * part)):
            start = pl.multiple_of(start, part)
            total = wide(own_ref, start, part) + wide(came_ref, start, part)
            for ref in refs[side * count : (side + 1) * count]:
                total = total + ref[...].astype(jnp.float32)
            refs[2 * count + side][...] = total.astype(jnp.bfloat16)

    return call(
        kernel,
        (bf16_rows(part, width), bf16_rows(part, width)),
        1 << 20,
        in_specs=[smem_spec()] + [vmem_spec()] * (2 + 2 * count),
        out_specs=(vmem_spec(), vmem_spec()),
    )(places, own, came, *arrived)


def per_device(
    frames,
    norm_gain,
    router,
    w_in,
    w_out,
    routing,
    head_gain,
    head_weight,
    frame_lengths,
    labels,
    label_lengths,
):
    sections = lax.axis_size("section")
    section_id = lax.axis_index("section")
    group_size = lax.axis_size("expert")
    member = lax.axis_index("expert")
    outer_size = lax.axis_size("dpo")
    inner_size = lax.axis_size("dpi")
    core = lax.axis_index("dpi")
    micro, utt_dev, frame_count, width = frames.shape
    label_max = labels.shape[2]
    experts = w_in.shape[1] * group_size
    pair_count = micro * utt_dev
    per_section = pair_count // sections
    first_pair = section_id * per_section
    share = (utt_dev * frame_count * 9 + 8 * experts - 1) // (8 * experts)
    group_count = 2 if per_section % (2 * utt_dev) == 0 else 1
    group_pairs = per_section // group_count
    filled = share * -(-group_pairs // utt_dev)
    capacity = round_up(filled + 1, 8)
    span = group_pairs * frame_count
    member_ref = member.astype(jnp.int32).reshape(1)

    def mine_of(value):
        return lax.dynamic_slice_in_dim(value, first_pair, per_section, 0)

    def exchange(blocks):
        return [blocks[0]] + [crossed(blocks[k], "expert", k) for k in range(1, group_size)]

    def lanes_of(ids):
        ids = jnp.pad(mine_of(ids), ((0, 0), (0, LANES - frame_count)), constant_values=-1)
        return [ids[g * group_pairs : (g + 1) * group_pairs] for g in range(group_count)]

    flat_frames = frames.reshape(pair_count * frame_count, width)
    current = [
        lax.dynamic_slice_in_dim(flat_frames, first_pair * frame_count + g * span, span, 0)
        for g in range(group_count)
    ]
    own_ids = routing.reshape(pair_count, frame_count)
    paired = sections == 2 and inner_size == 2
    if paired:
        other_ids = swap(own_ids, "section")
        all_ids = [
            jnp.where(section_id == layer, own_ids, other_ids) for layer in range(sections)
        ]
    else:
        all_ids = lax.all_gather(own_ids, "section")
    layer_ids = [lanes_of(all_ids[layer]) for layer in range(sections)]
    own_table = jnp.concatenate(
        [
            norm_gain,
            jnp.zeros((7, width), jnp.float32),
            jnp.transpose(router[0]).astype(jnp.float32),
            jnp.zeros((round_up(experts, 8) - experts, width), jnp.float32),
        ],
        axis=0,
    )
    own = (w_in[0, 0], w_out[0, 0])
    layers = []
    if paired:
        other_table = swap(own_table, "section")
    else:
        all_tables = lax.all_gather(own_table, "section")
        all_in = lax.all_gather(own[0], "section")
        all_out = lax.all_gather(own[1], "section")
        for layer in range(sections):
            chosen = (all_in[layer], all_out[layer])
            layers.append(((all_tables[layer],), chosen, [], jnp.ones((1,), jnp.int32)))

    outgoing = [
        dispatch(current[g], layer_ids[0][g], member_ref, experts, capacity, frame_count)
        for g in range(group_count)
    ]
    received = [exchange(blocks) for blocks in outgoing]
    if paired:
        sent_in, sent_out = half_weights(
            after(core.astype(jnp.int32).reshape(1), outgoing[0][0]), *own
        )
        came_in = swap(sent_in, "section")
        came_out = swap(sent_out, "section")
        came_in, came_out = lax.optimization_barrier((came_in, came_out, received))[:2]
        other = [(came_in, came_out), (swap(came_in, "dpi"), swap(came_out, "dpi"))]
        for layer in range(sections):
            mine = (section_id == layer).astype(jnp.int32).reshape(1)
            layers.append(((own_table, other_table), own, other, mine))

    notes = (
        first_pair.astype(jnp.int32).reshape(1),
        labels,
        jnp.transpose(frame_lengths),
        jnp.transpose(label_lengths),
    )
    shard = head_weight.shape[1]
    weight_rows = jnp.transpose(head_weight)
    line = group_size == 4
    tables = jnp.asarray(slot_tables(group_size, group_count))
    slots = lax.dynamic_index_in_dim(tables, member, 0, keepdims=False)
    outer = lax.axis_index("dpo")
    blocks = -(-shard // BLOCK_ROWS)
    tree = paired and outer_size == 2 and blocks == 8

    def pair_of(side, first, second):
        return [side * 4 + first, side * 4 + 2 + second]

    def offset_of(side, s, y):
        base = side * 4 * BLOCK_ROWS
        part = BLOCK_ROWS // 2
        return [
            base + s * BLOCK_ROWS + y * part,
            base + 2 * BLOCK_ROWS + y * BLOCK_ROWS + s * part,
        ]

    def whole_numbers(values):
        return jnp.stack([jnp.asarray(value, jnp.int32) for value in values])

    here, there = (section_id, outer), (1 - section_id, 1 - outer)
    sibling_order = whole_numbers(pair_of(1 - core, *there) + pair_of(1 - core, *here))
    sent_order = whole_numbers(pair_of(core, *there))
    kept_order = whole_numbers(pair_of(core, *here))
    chip_place = whole_numbers(here)
    first_offsets, last_offsets = [], offset_of(core, *there) + offset_of(1 - core, *there)
    for side in (core, 1 - core):
        for s, y in (here, (section_id, 1 - outer), (1 - section_id, outer)):
            first_offsets += offset_of(side, s, y)
    first_offsets, last_offsets = whole_numbers(first_offsets), whole_numbers(last_offsets)
    early = (
        slots,
        head_gain.reshape(1, width),
        layer_ids[1:],
        sibling_order,
        sent_order,
        kept_order,
        chip_place,
        first_offsets,
        last_offsets,
    )
    early, received = lax.optimization_barrier((early, received))
    slots, head_row, later_ids, sibling_order, sent_order, kept_order = early[:6]
    chip_place, first_offsets, last_offsets = early[6:]
    layer_ids = [layer_ids[0]] + list(later_ids)

    def tied(value, others, g):
        marks = [other for i, other in enumerate(others) if i != g]
        return after(value, *marks) if marks else value

    normed, marks = [], []
    for layer in range(sections):
        choices, weights, others, pick_own = layers[layer]
        done = [
            run_expert(
                received[g],
                choices,
                weights,
                others,
                tied(pick_own, marks, g),
                filled,
                notes if layer == 0 and g == 0 else None,
                per_section,
            )
            for g in range(group_count)
        ]
        returned = [exchange(parts) for parts in done]
        marks = [parts[0] for parts in done]
        tokens = [tied(member_ref, marks, g) for g in range(group_count)]
        if layer == sections - 1 and group_count > 1:
            tokens[-1] = after(tokens[-1], label_weight)
        sizes = (experts, capacity, frame_count)
        if layer < sections - 1:
            made = [
                combine_and_dispatch(
                    current[g],
                    returned[g],
                    layer_ids[layer][g],
                    choices,
                    pick_own,
                    layer_ids[layer + 1][g],
                    tokens[g],
                    *sizes,
                )
                for g in range(group_count)
            ]
            current = [pair[0] for pair in made]
            received = [exchange(pair[1]) for pair in made]
            marks = current
        else:
            normed = [
                combine_and_norm(
                    current[g],
                    returned[g],
                    layer_ids[layer][g],
                    choices,
                    pick_own,
                    head_row,
                    tokens[g],
                    *sizes,
                )
                for g in range(group_count)
            ]
        if layer == 0:
            found = list(returned[0])
            if not line:
                stacked = jnp.stack(found)
                found = [
                    lax.dynamic_index_in_dim(stacked, member ^ k, 0, keepdims=False)
                    for k in range(group_size)
                ]
            label_weight, places, names = label_rows(
                weight_rows, found, member_ref, group_count, group_pairs, filled, label_max, line
            )

    def logits_of(fill, first, count, pieces, earlier=None):
        return head_logits(
            fill, first, count, pieces, member_ref, weight_rows, label_weight, frame_count, earlier
        )

    def stats_of(stats):
        first = crossed(stats, "expert", 1)
        return [stats, first, crossed(stats, "expert", 2), crossed(first, "expert", 2)]

    heads, found = [], []
    for g in range(group_count):
        if line:
            beside = crossed(normed[g], "expert", 1)
            middle = lax.ppermute(normed[g], "expert", MIDDLE)
            beside, middle = lax.optimization_barrier((beside, middle, normed[-1]))[:2]
            far = lax.ppermute(beside, "expert", MIDDLE)
            outward = lax.ppermute(middle, "expert", OUTWARD)
            if g > 0:
                far = after(far, heads[0][2])
            last = lax.ppermute(far, "expert", OUTWARD)
            pieces = [normed[g], beside, middle, outward, far, last]
            earlier = heads[-1][2] if heads else None
            heads.append(logits_of(fill_line, g * group_size, group_size, pieces, earlier))
        else:
            gathered = lax.all_gather(normed[g], "expert")
            pieces = [gathered[k] for k in range(group_size)]
            heads.append(logits_of(fill_all, g * group_size, group_size, pieces))
            gathered = lax.all_gather(heads[g][2], "expert")
            found.append(
                [
                    lax.dynamic_index_in_dim(gathered, member ^ k, 0, keepdims=False)
                    for k in range(group_size)
                ]
            )
    if line:
        found = [stats_of(heads[-1][2])]
    kept_losses = group_pairs if line else group_size * group_pairs
    occupancy, high, low, losses = ctc_pass(
        found, slots, names, frame_count, label_max, group_count, kept_losses
    )
    if not line:
        pairs = losses.reshape(group_count, group_size, group_pairs)
        losses = lax.dynamic_index_in_dim(pairs, member, 1).reshape(1, per_section)
    losses = jnp.transpose(losses)

    def gradient(order, outputs, each):
        return head_gradient(
            [head[0] for head in heads],
            [head[1] for head in heads],
            occupancy,
            high,
            low,
            places,
            order,
            outputs,
            each,
        )

    if tree:
        sibling_sent, sibling_kept = gradient(sibling_order, 2, 2)
        came_sent, came_kept = swap(sibling_sent, "dpi"), swap(sibling_kept, "dpi")
        own_sent = gradient(after(sent_order, sibling_sent), 1, 2)[0]
        a_far, a_near, b_far, b_near = sum_sent(own_sent, came_sent, chip_place)
        kept_order = after(kept_order, a_far)
        a_far, b_far = swap(a_far, "section"), swap(b_far, "dpo")
        a_near, b_near = swap(a_near, "section"), swap(b_near, "dpo")
        own_kept = gradient(kept_order, 1, 2)[0]
        a_on, b_on = sum_kept(own_kept, came_kept, [a_far, b_far], chip_place, False)
        a_in, b_in = swap(a_on, "dpo"), swap(b_on, "section")
        a, b = sum_kept(own_kept, came_kept, [a_near, a_in, b_near, b_in], chip_place, True)
        a_y, b_x = swap(a, "dpo"), swap(b, "section")
        b_y, a_x = swap(b, "dpo"), swap(a, "section")
        a_xy, b_xy = swap(a_y, "section"), swap(b_x, "dpo")
        b_y, a_x = lax.optimization_barrier((b_y, a_x, a_xy, b_xy))[:2]
        mine = [a, b, a_y, b_y, a_x, b_x]
        theirs = [swap(value, "dpi") for value in mine]
        whole = assemble(mine + theirs, first_offsets, shard)
        last = [a_xy, b_xy, swap(a_xy, "dpi"), swap(b_xy, "dpi")]
        whole = assemble(last, last_offsets, shard, whole)
    else:
        partial = gradient(jnp.arange(blocks, dtype=jnp.int32), 1, blocks)[0][:shard]
        whole = lax.psum(partial.astype(jnp.float32), ("section", "dpo", "dpi")).astype(
            jnp.bfloat16
        )
    return (losses, jnp.transpose(whole))


def solution(mesh):
    sections, group_size, spread = (mesh.shape[name] for name in ("section", "expert", "dp"))
    inner = 2 if spread % 2 == 0 else 1
    split = Mesh(
        mesh.devices.reshape(sections, group_size, spread // inner, inner),
        ("section", "expert", "dpo", "dpi"),
    )
    block = ("expert", "dpo", "dpi")
    placed = (
        P(None, block, None, None),
        P("section", None),
        P("section", None, None),
        P("section", "expert", None, None),
        P("section", "expert", None, None),
        P("section", None, block, None, None),
        P(),
        P(None, "expert"),
        P(None, block),
        P(None, block, None),
        P(None, block),
    )
    return jax.shard_map(
        per_device,
        mesh=split,
        in_specs=placed,
        out_specs=(P("section", block), P(None, "expert")),
        check_vma=False,
    )
```

profile of v0, /device:TPU:0, one launch (start us, length us, event | category | flops | bytes accessed | tf_op | source)
XLA Modules:
  0.0 209.0 jit_solution(2662441690866163072)
XLA Ops:
  0.7 3.0 %collective-permute-start = (s32[8,48]{1,0:T(8,128)}, s32[8,48]{1,0:T(8,128)S(1)}, u32[]{:S(2)}, u32[]{:S(2)}) collective-permute-start(s32[8,48]{1,0:T(8,128)} %bitcast.64), channel_id=1, source_target_pairs={{0,16},{16,0},{1,17},{17,1},{2,18},{18,2},{3,19},{19,3},{4,20},{20... | collective-permute-start | bytes 4616 | tf_op jit(solution)/shard_map/ppermute | solution.py:741
  11.6 2.6 %collective-permute-start.2 = (bf16[32,1280]{1,0:T(8,128)(2,1)S(1)}, bf16[32,1280]{1,0:T(8,128)(2,1)S(1)}, u32[]{:S(2)}, u32[]{:S(2)}) collective-permute-start(bf16[32,1280]{1,0:T(8,128)(2,1)S(1)} %get-tuple-element.100), channel_id=1, source_target_pairs={{0,8},{4,12},{8,0},{12,4},{1,9},{5,13},{9,1},{13,5},{2,10},{6,14},... | collective-permute-start | bytes 245768 | tf_op jit(solution)/shard_map/ppermute | solution.py:746
  37.2 2.4 %collective-permute-start.16 = (bf16[32,1280]{1,0:T(8,128)(2,1)S(1)}, bf16[32,1280]{1,0:T(8,128)(2,1)S(1)}, u32[]{:S(2)}, u32[]{:S(2)}) collective-permute-start(bf16[32,1280]{1,0:T(8,128)(2,1)S(1)} %get-tuple-element.130), channel_id=1, source_target_pairs={{0,8},{4,12},{8,0},{12,4},{1,9},{5,13},{9,1},{13,5},{2,10},{6,14},... | collective-permute-start | bytes 245768 | tf_op jit(solution)/shard_map/ppermute | solution.py:746
  45.0 5.5 %collective-permute-start.18 = (bf16[32,1280]{1,0:T(8,128)(2,1)}, bf16[32,1280]{1,0:T(8,128)(2,1)S(1)}, u32[]{:S(2)}, u32[]{:S(2)}) collective-permute-start(bf16[32,1280]{1,0:T(8,128)(2,1)} %get-tuple-element.137), channel_id=1, source_target_pairs={{0,4},{4,0},{8,12},{12,8},{1,5},{5,1},{9,13},{13,9},{2,6},{6,2},{1... | collective-permute-start | bytes 245768 | tf_op jit(solution)/shard_map/ppermute | solution.py:746
  66.1 2.3 %collective-permute-done.22.refs_8_ = bf16[32,1280]{1,0:T(8,128)(2,1)S(1)} collective-permute-done((bf16[32,1280]{1,0:T(8,128)(2,1)}, bf16[32,1280]{1,0:T(8,128)(2,1)S(1)}, u32[]{:S(2)}, u32[]{:S(2)}) %collective-permute-start.22) | collective-permute-done | bytes 81952 | tf_op jit(solution)/shard_map/ppermute | solution.py:746
  69.2 4.1 %collective-permute-done.32.refs_4_ = bf16[32,1280]{1,0:T(8,128)(2,1)S(1)} collective-permute-done((bf16[32,1280]{1,0:T(8,128)(2,1)S(1)}, bf16[32,1280]{1,0:T(8,128)(2,1)S(1)}, u32[]{:S(2)}, u32[]{:S(2)}) %collective-permute-start.32) | collective-permute-done | bytes 81952 | tf_op jit(solution)/shard_map/ppermute | solution.py:746
  76.5 3.3 %collective-permute-start.24 = (bf16[32,1280]{1,0:T(8,128)(2,1)S(1)}, bf16[32,1280]{1,0:T(8,128)(2,1)S(1)}, u32[]{:S(2)}, u32[]{:S(2)}) collective-permute-start(bf16[32,1280]{1,0:T(8,128)(2,1)S(1)} %get-tuple-element.151), channel_id=1, source_target_pairs={{0,4},{4,0},{8,12},{12,8},{1,5},{5,1},{9,13},{13,9},{2,6},{6,2},{1... | collective-permute-start | bytes 245768 | tf_op jit(solution)/shard_map/ppermute | solution.py:746
  79.9 2.3 %collective-permute-start.26 = (bf16[32,1280]{1,0:T(8,128)(2,1)S(1)}, bf16[32,1280]{1,0:T(8,128)(2,1)S(1)}, u32[]{:S(2)}, u32[]{:S(2)}) collective-permute-start(bf16[32,1280]{1,0:T(8,128)(2,1)S(1)} %get-tuple-element.153), channel_id=1, source_target_pairs={{0,12},{4,8},{8,4},{12,0},{1,13},{5,9},{9,5},{13,1},{2,14},{6,10},... | collective-permute-start | bytes 245768 | tf_op jit(solution)/shard_map/ppermute | solution.py:746
  82.2 2.4 %copy-done.2 = bf16[1280,2000]{0,1:T(8,128)(2,1)S(1)} copy-done((bf16[1280,2000]{0,1:T(8,128)(2,1)S(1)}, bf16[1280,2000]{0,1:T(8,128)(2,1)}, u32[]{:S(2)}) %copy-start.2) | copy-done | bytes 5120024
  86.5 3.4 %collective-permute-done.25.refs_4_ = bf16[32,1280]{1,0:T(8,128)(2,1)S(1)} collective-permute-done((bf16[32,1280]{1,0:T(8,128)(2,1)S(1)}, bf16[32,1280]{1,0:T(8,128)(2,1)S(1)}, u32[]{:S(2)}, u32[]{:S(2)}) %collective-permute-start.25) | collective-permute-done | bytes 81952 | tf_op jit(solution)/shard_map/ppermute | solution.py:746
  91.5 4.5 %collective-permute-start.27 = (bf16[96,1280]{1,0:T(8,128)(2,1)S(1)}, bf16[96,1280]{1,0:T(8,128)(2,1)S(1)}, u32[]{:S(2)}, u32[]{:S(2)}) collective-permute-start(bf16[96,1280]{1,0:T(8,128)(2,1)S(1)} %shard_map.141.refs_0_), channel_id=1, source_target_pairs={{0,4},{4,0},{8,12},{12,8},{1,5},{5,1},{9,13},{13,9},{2,6},{6,2},{1... | collective-permute-start | bytes 737288 | tf_op jit(solution)/shard_map/ppermute | solution.py:746
  99.2 2.6 %collective-permute-done.27.refs_1_ = bf16[96,1280]{1,0:T(8,128)(2,1)S(1)} collective-permute-done((bf16[96,1280]{1,0:T(8,128)(2,1)S(1)}, bf16[96,1280]{1,0:T(8,128)(2,1)S(1)}, u32[]{:S(2)}, u32[]{:S(2)}) %collective-permute-start.27) | collective-permute-done | bytes 245792 | tf_op jit(solution)/shard_map/ppermute | solution.py:746
  103.8 3.6 %collective-permute-done.36.refs_3_ = bf16[96,1280]{1,0:T(8,128)(2,1)S(1)} collective-permute-done((bf16[96,1280]{1,0:T(8,128)(2,1)S(1)}, bf16[96,1280]{1,0:T(8,128)(2,1)S(1)}, u32[]{:S(2)}, u32[]{:S(2)}) %collective-permute-start.36) | collective-permute-done | bytes 245792 | tf_op jit(solution)/shard_map/ppermute | solution.py:1067
  107.4 5.3 %collective-permute-done.38.refs_5_ = bf16[96,1280]{1,0:T(8,128)(2,1)S(1)} collective-permute-done((bf16[96,1280]{1,0:T(8,128)(2,1)S(1)}, bf16[96,1280]{1,0:T(8,128)(2,1)S(1)}, u32[]{:S(2)}, u32[]{:S(2)}) %collective-permute-start.38) | collective-permute-done | bytes 245792 | tf_op jit(solution)/shard_map/ppermute | solution.py:1070
  112.7 3.2 %shard_map.143 = (f32[2048,384]{1,0:T(8,128)S(1)}, bf16[384,1280]{1,0:T(8,128)(2,1)S(1)}, f32[4,16,96]{2,1,0:T(8,128)S(1)}) custom-call(s32[1]{0:T(128)} %bitcast.28.member_ref, bf16[2000,1280]{1,0:T(8,128)(2,1)S(1)} %bitcast.58, bf16[256,1280]{1,0:T(8,128)(2,1)S(1)} %get-tuple-element.121.label_ref, bf16[96,1280]{1,0:T(8,128)(2,1)S(1)} %shard_map.142.refs_0_, ...), custom_call_target="tpu_custom_call" | custom-call | flops 2013265920 | tf_op jit(solution)/shard_map/pallas_call | solution.py:441
  117.2 6.8 %collective-permute-done.39.refs_5_ = bf16[96,1280]{1,0:T(8,128)(2,1)S(1)} collective-permute-done((bf16[96,1280]{1,0:T(8,128)(2,1)S(1)}, bf16[96,1280]{1,0:T(8,128)(2,1)S(1)}, u32[]{:S(2)}, u32[]{:S(2)}) %collective-permute-start.39) | collective-permute-done | bytes 245792 | tf_op jit(solution)/shard_map/ppermute | solution.py:1070
  124.0 3.2 %shard_map.144 = (f32[2048,384]{1,0:T(8,128)S(1)}, bf16[384,1280]{1,0:T(8,128)(2,1)S(1)}, f32[8,16,96]{2,1,0:T(8,128)S(1)}) custom-call(s32[1]{0:T(128)} %bitcast.28.member_ref, bf16[2000,1280]{1,0:T(8,128)(2,1)S(1)} %bitcast.59, bf16[256,1280]{1,0:T(8,128)(2,1)S(1)} %get-tuple-element.121.label_ref, bf16[96,1280]{1,0:T(8,128)(2,1)S(1)} %shard_map.141.refs_0_, ...), custom_call_target="tpu_custom_call" | custom-call | flops 2013265920 | tf_op jit(solution)/shard_map/pallas_call | solution.py:441
  128.7 2.8 %collective-permute-done.40.refs_1_ = f32[8,16,96]{2,1,0:T(8,128)S(1)} collective-permute-done((f32[8,16,96]{2,1,0:T(8,128)S(1)}, f32[8,16,96]{2,1,0:T(8,128)S(1)}, u32[]{:S(2)}, u32[]{:S(2)}) %collective-permute-start.40) | collective-permute-done | bytes 49184 | tf_op jit(solution)/shard_map/ppermute | solution.py:746
  132.5 4.3 %collective-permute-done.42.refs_3_ = f32[8,16,96]{2,1,0:T(8,128)S(1)} collective-permute-done((f32[8,16,96]{2,1,0:T(8,128)S(1)}, f32[8,16,96]{2,1,0:T(8,128)S(1)}, u32[]{:S(2)}, u32[]{:S(2)}) %collective-permute-start.42) | collective-permute-done | bytes 49184 | tf_op jit(solution)/shard_map/ppermute | solution.py:746
  136.8 7.1 %shard_map.145 = (f32[16,768]{1,0:T(8,128)S(1)}, bf16[256,768]{1,0:T(8,128)(2,1)S(1)}, bf16[256,768]{1,0:T(8,128)(2,1)S(1)}, f32[1,4]{1,0:T(1,128)}) custom-call(s32[32]{0:T(128)S(1)} %copy-done.19, s32[16,128]{1,0:T(8,128)S(1)} %get-tuple-element.120.notes_ref, f32[8,16,96]{2,1,0:T(8,128)S(1)} %get-tuple-element.164.refs_0_, ...), custom_call_target="tpu_custom_call" | custom-call | flops 67108864 | tf_op jit(solution)/shard_map/pallas_call | solution.py:632
  144.0 4.9 %shard_map.146 = (bf16[512,1280]{1,0:T(8,128)(2,1)S(1)}, bf16[512,1280]{1,0:T(8,128)(2,1)S(1)}) custom-call(s32[4]{0:T(128)S(1)} %copy-done.20, f32[2048,384]{1,0:T(8,128)S(1)} %get-tuple-element.171.refs_0_, f32[2048,384]{1,0:T(8,128)S(1)} %get-tuple-element.172.refs_1_, bf16[384,1280]{1,0:T(8,128)(2,1)S(1)} %get-tuple-element.173.refs_2_, ...), custom_call_target="tpu_custom_call" | custom-call | flops 2818572288 | tf_op jit(solution)/shard_map/pallas_call | solution.py:683
  149.5 2.8 %shard_map.147.own_ref = bf16[512,1280]{1,0:T(8,128)(2,1)S(1)} custom-call(s32[2]{0:T(128)S(1)} %get-tuple-element.180.order_ref, f32[2048,384]{1,0:T(8,128)S(1)} %get-tuple-element.171.refs_0_, f32[2048,384]{1,0:T(8,128)S(1)} %get-tuple-element.172.refs_1_, bf16[384,1280]{1,0:T(8,128)(2,1)S(1)} %get-tuple-element.173.refs_2_, ...), custom_call_target="tpu_custom_call" | custom-call | flops 1409286144 | tf_op jit(solution)/shard_map/pallas_call | solution.py:683
  154.8 2.0 collective-permute-start.45
  157.3 2.8 %shard_map.149.own_ref = bf16[512,1280]{1,0:T(8,128)(2,1)S(1)} custom-call(s32[2]{0:T(128)S(1)} %get-tuple-element.182.order_ref, f32[2048,384]{1,0:T(8,128)S(1)} %get-tuple-element.171.refs_0_, f32[2048,384]{1,0:T(8,128)S(1)} %get-tuple-element.172.refs_1_, bf16[384,1280]{1,0:T(8,128)(2,1)S(1)} %get-tuple-element.173.refs_2_, ...), custom_call_target="tpu_custom_call" | custom-call | flops 1409286144 | tf_op jit(solution)/shard_map/pallas_call | solution.py:683
  160.1 3.7 %collective-permute-done.46.refs_0_ = bf16[128,1280]{1,0:T(8,128)(2,1)S(1)} collective-permute-done((bf16[128,1280]{1,0:T(8,128)(2,1)S(1)}, bf16[128,1280]{1,0:T(8,128)(2,1)S(1)}, u32[]{:S(2)}, u32[]{:S(2)}) %collective-permute-start.46) | collective-permute-done | bytes 327712 | tf_op jit(solution)/shard_map/ppermute | solution.py:741
  166.2 2.0 collective-permute-start.50
  168.2 2.6 %collective-permute-done.45.refs_0_ = bf16[128,1280]{1,0:T(8,128)(2,1)S(1)} collective-permute-done((bf16[128,1280]{1,0:T(8,128)(2,1)S(1)}, bf16[128,1280]{1,0:T(8,128)(2,1)S(1)}, u32[]{:S(2)}, u32[]{:S(2)}) %collective-permute-start.45) | collective-permute-done | bytes 327712 | tf_op jit(solution)/shard_map/ppermute | solution.py:741
  170.9 6.1 %collective-permute-done.48.refs_1_ = bf16[128,1280]{1,0:T(8,128)(2,1)S(1)} collective-permute-done((bf16[128,1280]{1,0:T(8,128)(2,1)S(1)}, bf16[128,1280]{1,0:T(8,128)(2,1)S(1)}, u32[]{:S(2)}, u32[]{:S(2)}) %collective-permute-start.48) | collective-permute-done | bytes 327712 | tf_op jit(solution)/shard_map/ppermute | solution.py:741
  182.0 6.6 %collective-permute-done.51.refs_2_ = bf16[128,1280]{1,0:T(8,128)(2,1)S(1)} collective-permute-done((bf16[128,1280]{1,0:T(8,128)(2,1)S(1)}, bf16[128,1280]{1,0:T(8,128)(2,1)S(1)}, u32[]{:S(2)}, u32[]{:S(2)}) %collective-permute-start.51) | collective-permute-done | bytes 327712 | tf_op jit(solution)/shard_map/ppermute | solution.py:741
  191.8 3.8 %collective-permute-done.57.refs_3_ = bf16[128,1280]{1,0:T(8,128)(2,1)S(1)} collective-permute-done((bf16[128,1280]{1,0:T(8,128)(2,1)S(1)}, bf16[128,1280]{1,0:T(8,128)(2,1)S(1)}, u32[]{:S(2)}, u32[]{:S(2)}) %collective-permute-start.57) | collective-permute-done | bytes 327712 | tf_op jit(solution)/shard_map/ppermute | solution.py:741
  197.2 4.9 %collective-permute-done.52.refs_0_ = bf16[128,1280]{1,0:T(8,128)(2,1)S(1)} collective-permute-done((bf16[128,1280]{1,0:T(8,128)(2,1)S(1)}, bf16[128,1280]{1,0:T(8,128)(2,1)S(1)}, u32[]{:S(2)}, u32[]{:S(2)}) %collective-permute-start.52) | collective-permute-done | bytes 327712 | tf_op jit(solution)/shard_map/ppermute | solution.py:741
  204.7 2.6 %shard_map.152.refs_4_ = bf16[2000,1280]{1,0:T(8,128)(2,1)} custom-call(s32[12]{0:T(128)S(1)} %stack.122.offsets_ref, bf16[128,1280]{1,0:T(8,128)(2,1)S(1)} %get-tuple-element.189.refs_0_, bf16[128,1280]{1,0:T(8,128)(2,1)S(1)} %get-tuple-element.190.refs_1_, bf16[128,1280]{1,0:T(8,128)(2,1)S(1)} %collective-permute-done.51.refs_2_, ...), custom_call_target="tpu_custom_call" | custom-call | tf_op jit(solution)/shard_map/pallas_call | solution.py:730
  (198 shorter events, 88.0 us)
Async XLA Ops:
  7.4 20.1 %collective-permute-start.8 = (bf16[1280,128]{1,0:T(8,128)(2,1)S(1)}, bf16[1280,128]{1,0:T(8,128)(2,1)S(1)}, u32[]{:S(2)}, u32[]{:S(2)}) collective-permute-start(bf16[1280,128]{1,0:T(8,128)(2,1)S(1)} %get-tuple-element.108), channel_id=1, source_target_pairs={{0,16},{16,0},{1,17},{17,1},{2,18},{18,2},{3,19},{19,3},{4,20},{20... | collective-permute-start | bytes 983048 | tf_op jit(solution)/shard_map/ppermute | solution.py:741
  9.2 18.3 %collective-permute-start.9 = (bf16[128,1280]{1,0:T(8,128)(2,1)S(1)}, bf16[128,1280]{1,0:T(8,128)(2,1)S(1)}, u32[]{:S(2)}, u32[]{:S(2)}) collective-permute-start(bf16[128,1280]{1,0:T(8,128)(2,1)S(1)} %get-tuple-element.109), channel_id=1, source_target_pairs={{0,16},{16,0},{1,17},{17,1},{2,18},{18,2},{3,19},{19,3},{4,20},{20... | collective-permute-start | bytes 983048 | tf_op jit(solution)/shard_map/ppermute | solution.py:741
  36.6 14.7 %collective-permute-start.15 = (bf16[32,1280]{1,0:T(8,128)(2,1)S(1)}, bf16[32,1280]{1,0:T(8,128)(2,1)S(1)}, u32[]{:S(2)}, u32[]{:S(2)}) collective-permute-start(bf16[32,1280]{1,0:T(8,128)(2,1)S(1)} %get-tuple-element.129), channel_id=1, source_target_pairs={{0,4},{4,0},{8,12},{12,8},{1,5},{5,1},{9,13},{13,9},{2,6},{6,2},{1... | collective-permute-start | bytes 245768 | tf_op jit(solution)/shard_map/ppermute | solution.py:746
  37.2 15.7 %collective-permute-start.16 = (bf16[32,1280]{1,0:T(8,128)(2,1)S(1)}, bf16[32,1280]{1,0:T(8,128)(2,1)S(1)}, u32[]{:S(2)}, u32[]{:S(2)}) collective-permute-start(bf16[32,1280]{1,0:T(8,128)(2,1)S(1)} %get-tuple-element.130), channel_id=1, source_target_pairs={{0,8},{4,12},{8,0},{12,4},{1,9},{5,13},{9,1},{13,5},{2,10},{6,14},... | collective-permute-start | bytes 245768 | tf_op jit(solution)/shard_map/ppermute | solution.py:746
  39.6 13.3 %collective-permute-start.17 = (bf16[32,1280]{1,0:T(8,128)(2,1)S(1)}, bf16[32,1280]{1,0:T(8,128)(2,1)S(1)}, u32[]{:S(2)}, u32[]{:S(2)}) collective-permute-start(bf16[32,1280]{1,0:T(8,128)(2,1)S(1)} %get-tuple-element.131), channel_id=1, source_target_pairs={{0,12},{4,8},{8,4},{12,0},{1,13},{5,9},{9,5},{13,1},{2,14},{6,10},... | collective-permute-start | bytes 245768 | tf_op jit(solution)/shard_map/ppermute | solution.py:746
  45.0 14.2 %collective-permute-start.18 = (bf16[32,1280]{1,0:T(8,128)(2,1)}, bf16[32,1280]{1,0:T(8,128)(2,1)S(1)}, u32[]{:S(2)}, u32[]{:S(2)}) collective-permute-start(bf16[32,1280]{1,0:T(8,128)(2,1)} %get-tuple-element.137), channel_id=1, source_target_pairs={{0,4},{4,0},{8,12},{12,8},{1,5},{5,1},{9,13},{13,9},{2,6},{6,2},{1... | collective-permute-start | bytes 245768 | tf_op jit(solution)/shard_map/ppermute | solution.py:746
  50.5 10.3 %collective-permute-start.19 = (bf16[32,1280]{1,0:T(8,128)(2,1)}, bf16[32,1280]{1,0:T(8,128)(2,1)S(1)}, u32[]{:S(2)}, u32[]{:S(2)}) collective-permute-start(bf16[32,1280]{1,0:T(8,128)(2,1)} %get-tuple-element.138), channel_id=1, source_target_pairs={{0,8},{4,12},{8,0},{12,4},{1,9},{5,13},{9,1},{13,5},{2,10},{6,14},... | collective-permute-start | bytes 245768 | tf_op jit(solution)/shard_map/ppermute | solution.py:746
  57.5 10.8 %collective-permute-start.22 = (bf16[32,1280]{1,0:T(8,128)(2,1)}, bf16[32,1280]{1,0:T(8,128)(2,1)S(1)}, u32[]{:S(2)}, u32[]{:S(2)}) collective-permute-start(bf16[32,1280]{1,0:T(8,128)(2,1)} %copy-done.23), channel_id=1, source_target_pairs={{0,8},{4,12},{8,0},{12,4},{1,9},{5,13},{9,1},{13,5},{2,10},{6,14},... | collective-permute-start | bytes 245768 | tf_op jit(solution)/shard_map/ppermute | solution.py:746
  63.2 10.1 %collective-permute-start.32 = (bf16[32,1280]{1,0:T(8,128)(2,1)S(1)}, bf16[32,1280]{1,0:T(8,128)(2,1)S(1)}, u32[]{:S(2)}, u32[]{:S(2)}) collective-permute-start(bf16[32,1280]{1,0:T(8,128)(2,1)S(1)} %get-tuple-element.158), channel_id=1, source_target_pairs={{0,8},{4,12},{8,0},{12,4},{1,9},{5,13},{9,1},{13,5},{2,10},{6,14},... | collective-permute-start | bytes 245768 | tf_op jit(solution)/shard_map/ppermute | solution.py:746
  74.1 16.7 %collective-permute-start.34 = (bf16[96,1280]{1,0:T(8,128)(2,1)S(1)}, bf16[96,1280]{1,0:T(8,128)(2,1)S(1)}, u32[]{:S(2)}, u32[]{:S(2)}) collective-permute-start(bf16[96,1280]{1,0:T(8,128)(2,1)S(1)} %shard_map.142.refs_0_), channel_id=1, source_target_pairs={{0,4},{4,0},{8,12},{12,8},{1,5},{5,1},{9,13},{13,9},{2,6},{6,2},{1... | collective-permute-start | bytes 737288 | tf_op jit(solution)/shard_map/ppermute | solution.py:746
  75.6 15.2 %collective-permute-start.35 = (bf16[96,1280]{1,0:T(8,128)(2,1)S(1)}, bf16[96,1280]{1,0:T(8,128)(2,1)S(1)}, u32[]{:S(2)}, u32[]{:S(2)}) collective-permute-start(bf16[96,1280]{1,0:T(8,128)(2,1)S(1)} %shard_map.142.refs_0_), channel_id=1, source_target_pairs={{4,8},{8,4},{5,9},{9,5},{6,10},{10,6},{7,11},{11,7},{20,24},{24,20... | collective-permute-start | bytes 737288 | tf_op jit(solution)/shard_map/ppermute | solution.py:1064
  76.5 10.1 %collective-permute-start.24 = (bf16[32,1280]{1,0:T(8,128)(2,1)S(1)}, bf16[32,1280]{1,0:T(8,128)(2,1)S(1)}, u32[]{:S(2)}, u32[]{:S(2)}) collective-permute-start(bf16[32,1280]{1,0:T(8,128)(2,1)S(1)} %get-tuple-element.151), channel_id=1, source_target_pairs={{0,4},{4,0},{8,12},{12,8},{1,5},{5,1},{9,13},{13,9},{2,6},{6,2},{1... | collective-permute-start | bytes 245768 | tf_op jit(solution)/shard_map/ppermute | solution.py:746
  79.7 10.2 %collective-permute-start.25 = (bf16[32,1280]{1,0:T(8,128)(2,1)S(1)}, bf16[32,1280]{1,0:T(8,128)(2,1)S(1)}, u32[]{:S(2)}, u32[]{:S(2)}) collective-permute-start(bf16[32,1280]{1,0:T(8,128)(2,1)S(1)} %get-tuple-element.152), channel_id=1, source_target_pairs={{0,8},{4,12},{8,0},{12,4},{1,9},{5,13},{9,1},{13,5},{2,10},{6,14},... | collective-permute-start | bytes 245768 | tf_op jit(solution)/shard_map/ppermute | solution.py:746
  91.5 10.4 %collective-permute-start.27 = (bf16[96,1280]{1,0:T(8,128)(2,1)S(1)}, bf16[96,1280]{1,0:T(8,128)(2,1)S(1)}, u32[]{:S(2)}, u32[]{:S(2)}) collective-permute-start(bf16[96,1280]{1,0:T(8,128)(2,1)S(1)} %shard_map.141.refs_0_), channel_id=1, source_target_pairs={{0,4},{4,0},{8,12},{12,8},{1,5},{5,1},{9,13},{13,9},{2,6},{6,2},{1... | collective-permute-start | bytes 737288 | tf_op jit(solution)/shard_map/ppermute | solution.py:746
  96.6 10.8 %collective-permute-start.36 = (bf16[96,1280]{1,0:T(8,128)(2,1)S(1)}, bf16[96,1280]{1,0:T(8,128)(2,1)S(1)}, u32[]{:S(2)}, u32[]{:S(2)}) collective-permute-start(bf16[96,1280]{1,0:T(8,128)(2,1)S(1)} %collective-permute-done.35.refs_2_), channel_id=1, source_target_pairs={{4,0},{8,12},{5,1},{9,13},{6,2},{10,14},{7,3},{11,15},{20,16},{24,... | collective-permute-start | bytes 737288 | tf_op jit(solution)/shard_map/ppermute | solution.py:1067
  97.9 14.7 %collective-permute-start.38 = (bf16[96,1280]{1,0:T(8,128)(2,1)S(1)}, bf16[96,1280]{1,0:T(8,128)(2,1)S(1)}, u32[]{:S(2)}, u32[]{:S(2)}) collective-permute-start(bf16[96,1280]{1,0:T(8,128)(2,1)S(1)} %collective-permute-done.37.refs_4_), channel_id=1, source_target_pairs={{4,0},{8,12},{5,1},{9,13},{6,2},{10,14},{7,3},{11,15},{20,16},{24,... | collective-permute-start | bytes 737288 | tf_op jit(solution)/shard_map/ppermute | solution.py:1070
  101.9 14.0 %collective-permute-start.30 = (bf16[96,1280]{1,0:T(8,128)(2,1)S(1)}, bf16[96,1280]{1,0:T(8,128)(2,1)S(1)}, u32[]{:S(2)}, u32[]{:S(2)}) collective-permute-start(bf16[96,1280]{1,0:T(8,128)(2,1)S(1)} %collective-permute-done.27.refs_1_), channel_id=1, source_target_pairs={{4,8},{8,4},{5,9},{9,5},{6,10},{10,6},{7,11},{11,7},{20,24},{24,20... | collective-permute-start | bytes 737288 | tf_op jit(solution)/shard_map/ppermute | solution.py:1066
  102.5 14.7 %collective-permute-start.29 = (bf16[96,1280]{1,0:T(8,128)(2,1)S(1)}, bf16[96,1280]{1,0:T(8,128)(2,1)S(1)}, u32[]{:S(2)}, u32[]{:S(2)}) collective-permute-start(bf16[96,1280]{1,0:T(8,128)(2,1)S(1)} %collective-permute-done.28.refs_2_), channel_id=1, source_target_pairs={{4,0},{8,12},{5,1},{9,13},{6,2},{10,14},{7,3},{11,15},{20,16},{24,... | collective-permute-start | bytes 737288 | tf_op jit(solution)/shard_map/ppermute | solution.py:1067
  149.0 11.1 %collective-permute-start.44 = (bf16[512,1280]{1,0:T(8,128)(2,1)S(1)}, bf16[512,1280]{1,0:T(8,128)(2,1)S(1)}, u32[]{:S(2)}, u32[]{:S(2)}) collective-permute-start(bf16[512,1280]{1,0:T(8,128)(2,1)S(1)} %get-tuple-element.183), channel_id=1, source_target_pairs={{0,1},{1,0},{2,3},{3,2},{4,5},{5,4},{6,7},{7,6},{8,9},{9,8},{10,11... | collective-permute-start | bytes 3932168 | tf_op jit(solution)/shard_map/ppermute | solution.py:741
  153.1 10.6 %collective-permute-start.46 = (bf16[128,1280]{1,0:T(8,128)(2,1)S(1)}, bf16[128,1280]{1,0:T(8,128)(2,1)S(1)}, u32[]{:S(2)}, u32[]{:S(2)}) collective-permute-start(bf16[128,1280]{1,0:T(8,128)(2,1)S(1)} %get-tuple-element.181), channel_id=1, source_target_pairs={{0,16},{16,0},{1,17},{17,1},{2,18},{18,2},{3,19},{19,3},{4,20},{20... | collective-permute-start | bytes 983048 | tf_op jit(solution)/shard_map/ppermute | solution.py:741
  153.2 10.6 %collective-permute-start.47 = (bf16[128,1280]{1,0:T(8,128)(2,1)S(1)}, bf16[128,1280]{1,0:T(8,128)(2,1)S(1)}, u32[]{:S(2)}, u32[]{:S(2)}) collective-permute-start(bf16[128,1280]{1,0:T(8,128)(2,1)S(1)} %get-tuple-element.185), channel_id=1, source_target_pairs={{0,2},{2,0},{1,3},{3,1},{4,6},{6,4},{5,7},{7,5},{8,10},{10,8},{9,1... | collective-permute-start | bytes 983048 | tf_op jit(solution)/shard_map/ppermute | solution.py:741
  154.8 16.0 %collective-permute-start.45 = (bf16[128,1280]{1,0:T(8,128)(2,1)S(1)}, bf16[128,1280]{1,0:T(8,128)(2,1)S(1)}, u32[]{:S(2)}, u32[]{:S(2)}) collective-permute-start(bf16[128,1280]{1,0:T(8,128)(2,1)S(1)} %get-tuple-element.184), channel_id=1, source_target_pairs={{0,16},{16,0},{1,17},{17,1},{2,18},{18,2},{3,19},{19,3},{4,20},{20... | collective-permute-start | bytes 983048 | tf_op jit(solution)/shard_map/ppermute | solution.py:741
  156.8 14.1 %collective-permute-start.49 = (bf16[128,1280]{1,0:T(8,128)(2,1)S(1)}, bf16[128,1280]{1,0:T(8,128)(2,1)S(1)}, u32[]{:S(2)}, u32[]{:S(2)}) collective-permute-start(bf16[128,1280]{1,0:T(8,128)(2,1)S(1)} %get-tuple-element.187), channel_id=1, source_target_pairs={{0,2},{2,0},{1,3},{3,1},{4,6},{6,4},{5,7},{7,5},{8,10},{10,8},{9,1... | collective-permute-start | bytes 983048 | tf_op jit(solution)/shard_map/ppermute | solution.py:741
  164.6 12.4 %collective-permute-start.48 = (bf16[128,1280]{1,0:T(8,128)(2,1)S(1)}, bf16[128,1280]{1,0:T(8,128)(2,1)S(1)}, u32[]{:S(2)}, u32[]{:S(2)}) collective-permute-start(bf16[128,1280]{1,0:T(8,128)(2,1)S(1)} %get-tuple-element.186), channel_id=1, source_target_pairs={{0,2},{2,0},{1,3},{3,1},{4,6},{6,4},{5,7},{7,5},{8,10},{10,8},{9,1... | collective-permute-start | bytes 983048 | tf_op jit(solution)/shard_map/ppermute | solution.py:741
  166.2 10.8 %collective-permute-start.50 = (bf16[128,1280]{1,0:T(8,128)(2,1)S(1)}, bf16[128,1280]{1,0:T(8,128)(2,1)S(1)}, u32[]{:S(2)}, u32[]{:S(2)}) collective-permute-start(bf16[128,1280]{1,0:T(8,128)(2,1)S(1)} %get-tuple-element.188), channel_id=1, source_target_pairs={{0,16},{16,0},{1,17},{17,1},{2,18},{18,2},{3,19},{19,3},{4,20},{20... | collective-permute-start | bytes 983048 | tf_op jit(solution)/shard_map/ppermute | solution.py:741
  177.9 10.7 %collective-permute-start.51 = (bf16[128,1280]{1,0:T(8,128)(2,1)S(1)}, bf16[128,1280]{1,0:T(8,128)(2,1)S(1)}, u32[]{:S(2)}, u32[]{:S(2)}) collective-permute-start(bf16[128,1280]{1,0:T(8,128)(2,1)S(1)} %get-tuple-element.189.refs_0_), channel_id=1, source_target_pairs={{0,2},{2,0},{1,3},{3,1},{4,6},{6,4},{5,7},{7,5},{8,10},{10,8},{9,1... | collective-permute-start | bytes 983048 | tf_op jit(solution)/shard_map/ppermute | solution.py:741
  179.5 10.8 %collective-permute-start.53 = (bf16[128,1280]{1,0:T(8,128)(2,1)S(1)}, bf16[128,1280]{1,0:T(8,128)(2,1)S(1)}, u32[]{:S(2)}, u32[]{:S(2)}) collective-permute-start(bf16[128,1280]{1,0:T(8,128)(2,1)S(1)} %get-tuple-element.190.refs_1_), channel_id=1, source_target_pairs={{0,16},{16,0},{1,17},{17,1},{2,18},{18,2},{3,19},{19,3},{4,20},{20... | collective-permute-start | bytes 983048 | tf_op jit(solution)/shard_map/ppermute | solution.py:741
  181.2 14.5 %collective-permute-start.57 = (bf16[128,1280]{1,0:T(8,128)(2,1)S(1)}, bf16[128,1280]{1,0:T(8,128)(2,1)S(1)}, u32[]{:S(2)}, u32[]{:S(2)}) collective-permute-start(bf16[128,1280]{1,0:T(8,128)(2,1)S(1)} %get-tuple-element.190.refs_1_), channel_id=1, source_target_pairs={{0,2},{2,0},{1,3},{3,1},{4,6},{6,4},{5,7},{7,5},{8,10},{10,8},{9,1... | collective-permute-start | bytes 983048 | tf_op jit(solution)/shard_map/ppermute | solution.py:741
  181.7 15.5 %collective-permute-start.58 = (bf16[128,1280]{1,0:T(8,128)(2,1)S(1)}, bf16[128,1280]{1,0:T(8,128)(2,1)S(1)}, u32[]{:S(2)}, u32[]{:S(2)}) collective-permute-start(bf16[128,1280]{1,0:T(8,128)(2,1)S(1)} %get-tuple-element.189.refs_0_), channel_id=1, source_target_pairs={{0,16},{16,0},{1,17},{17,1},{2,18},{18,2},{3,19},{19,3},{4,20},{20... | collective-permute-start | bytes 983048 | tf_op jit(solution)/shard_map/ppermute | solution.py:741
  188.6 13.5 %collective-permute-start.52 = (bf16[128,1280]{1,0:T(8,128)(2,1)S(1)}, bf16[128,1280]{1,0:T(8,128)(2,1)S(1)}, u32[]{:S(2)}, u32[]{:S(2)}) collective-permute-start(bf16[128,1280]{1,0:T(8,128)(2,1)S(1)} %collective-permute-done.51.refs_2_), channel_id=1, source_target_pairs={{0,16},{16,0},{1,17},{17,1},{2,18},{18,2},{3,19},{19,3},{4,20},{20... | collective-permute-start | bytes 983048 | tf_op jit(solution)/shard_map/ppermute | solution.py:741
  190.3 11.8 %collective-permute-start.54 = (bf16[128,1280]{1,0:T(8,128)(2,1)S(1)}, bf16[128,1280]{1,0:T(8,128)(2,1)S(1)}, u32[]{:S(2)}, u32[]{:S(2)}) collective-permute-start(bf16[128,1280]{1,0:T(8,128)(2,1)S(1)} %collective-permute-done.53.refs_5_), channel_id=1, source_target_pairs={{0,2},{2,0},{1,3},{3,1},{4,6},{6,4},{5,7},{7,5},{8,10},{10,8},{9,1... | collective-permute-start | bytes 983048 | tf_op jit(solution)/shard_map/ppermute | solution.py:741
  191.8 10.8 %collective-permute-start.59 = (bf16[128,1280]{1,0:T(8,128)(2,1)S(1)}, bf16[128,1280]{1,0:T(8,128)(2,1)S(1)}, u32[]{:S(2)}, u32[]{:S(2)}) collective-permute-start(bf16[128,1280]{1,0:T(8,128)(2,1)S(1)} %get-tuple-element.189.refs_0_), channel_id=1, source_target_pairs={{0,1},{1,0},{2,3},{3,2},{4,5},{5,4},{6,7},{7,6},{8,9},{9,8},{10,11... | collective-permute-start | bytes 983048 | tf_op jit(solution)/shard_map/ppermute | solution.py:741
  (63 other events, 540.2 us)
where the time goes:
time: 209 us
  starting transfers between devices  79.7 us (38%)
  waiting for transfers between devices  75 us (36%)
  Pallas kernels  42.7 us (20%)
  local copies, waits for them, and re-layouts  7.77 us (4%)
  other arithmetic  2.29 us (1%)
    ppermute x29, starting transfers between devices, crossed(): return lax.ppermute(value, axis, [(i, i ^ by) for i in range(count)])  48.3 us
    ppermute x28, waiting for transfers between devices, swap(): return lax.ppermute(value, axis, [(0, 1), (1, 0)])  30.9 us
    ppermute x29, waiting for transfers between devices, crossed(): return lax.ppermute(value, axis, [(i, i ^ by) for i in range(count)])  28.5 us
    ppermute x28, starting transfers between devices, swap(): return lax.ppermute(value, axis, [(0, 1), (1, 0)])  23.4 us
    ppermute x2, waiting for transfers between devices, per_device(): last = lax.ppermute(far, 'expert', OUTWARD)  12 us
    pallas_call x3, Pallas kernels, head_gradient(): call(kernel, tuple((bf16_rows(each * BLOCK_ROWS, width) for _ in range(ou...  10.6 us
    pallas_call x1, Pallas kernels, ctc_pass(): call(kernel, (jax.ShapeDtypeStruct((COLS, row_count), jnp.float32), bf16_...  7.13 us
    pallas_call x2, Pallas kernels, head_logits(): call(kernel, (jax.ShapeDtypeStruct((height, row_count), jnp.float32), bf1...  6.4 us
  transfers between devices with their start and end apart: 65, of which 29 were waited for; matrix products, arithmetic and copies ran while one was open for 2% of the time, Pallas kernels for 10%

commit v1 on v0

--- a/solution.py
+++ b/solution.py
@@ -958,10 +958,12 @@
     sent_order = whole_numbers(pair_of(core, *there))
     kept_order = whole_numbers(pair_of(core, *here))
     chip_place = whole_numbers(here)
-    first_offsets, last_offsets = [], offset_of(core, *there) + offset_of(1 - core, *there)
+    first_offsets, last_offsets = [], []
     for side in (core, 1 - core):
-        for s, y in (here, (section_id, 1 - outer), (1 - section_id, outer)):
-            first_offsets += offset_of(side, s, y)
+        near_y = offset_of(side, section_id, 1 - outer)
+        near_x = offset_of(side, 1 - section_id, outer)
+        first_offsets += offset_of(side, *here) + [near_y[0], near_x[1]]
+        last_offsets += [near_y[1], near_x[0]] + offset_of(side, *there)
     first_offsets, last_offsets = whole_numbers(first_offsets), whole_numbers(last_offsets)
     early = (
         slots,
@@ -1122,11 +1124,12 @@
         b_y, a_x = swap(b, "dpo"), swap(a, "section")
         a_xy, b_xy = swap(a_y, "section"), swap(b_x, "dpo")
         b_y, a_x = lax.optimization_barrier((b_y, a_x, a_xy, b_xy))[:2]
-        mine = [a, b, a_y, b_y, a_x, b_x]
+        mine = [a, b, a_y, b_x]
         theirs = [swap(value, "dpi") for value in mine]
         whole = assemble(mine + theirs, first_offsets, shard)
-        last = [a_xy, b_xy, swap(a_xy, "dpi"), swap(b_xy, "dpi")]
-        whole = assemble(last, last_offsets, shard, whole)
+        mine = [b_y, a_x, a_xy, b_xy]
+        theirs = [swap(value, "dpi") for value in mine]
+        whole = assemble(mine + theirs, last_offsets, shard, whole)
     else:
         partial = gradient(jnp.arange(blocks, dtype=jnp.int32), 1, blocks)[0][:shard]
         whole = lax.psum(partial.astype(jnp.float32), ("section", "dpo", "dpi")).astype(

time: 209 us -> 210 us (level)
  transfers between devices with their start and end apart: 65 -> 65, of which waited for: 29 -> 28; matrix products, arithmetic and copies ran while one was open for 2% -> 3% of each run, Pallas kernels for 10% -> 10%
where the time goes in v1:
time: 210 us
  starting transfers between devices  78.1 us (37%)
  waiting for transfers between devices  74.6 us (36%)
  Pallas kernels  42.8 us (20%)
  local copies, waits for them, and re-layouts  9.08 us (4%)
  other arithmetic  3.53 us (2%)
    ppermute x29, starting transfers between devices, crossed(): return lax.ppermute(value, axis, [(i, i ^ by) for i in range(count)])  48.7 us
    ppermute x28, waiting for transfers between devices, swap(): return lax.ppermute(value, axis, [(0, 1), (1, 0)])  31.5 us
    ppermute x29, waiting for transfers between devices, crossed(): return lax.ppermute(value, axis, [(i, i ^ by) for i in range(count)])  27.3 us
    ppermute x28, starting transfers between devices, swap(): return lax.ppermute(value, axis, [(0, 1), (1, 0)])  21.4 us
    ppermute x2, waiting for transfers between devices, per_device(): last = lax.ppermute(far, 'expert', OUTWARD)  12 us
    pallas_call x3, Pallas kernels, head_gradient(): call(kernel, tuple((bf16_rows(each * BLOCK_ROWS, width) for _ in range(ou...  10.6 us
    pallas_call x1, Pallas kernels, ctc_pass(): call(kernel, (jax.ShapeDtypeStruct((COLS, row_count), jnp.float32), bf16_...  7.13 us
    pallas_call x2, Pallas kernels, head_logits(): call(kernel, (jax.ShapeDtypeStruct((height, row_count), jnp.float32), bf1...  6.48 us
  transfers between devices with their start and end apart: 65, of which 28 were waited for; matrix products, arithmetic and copies ran while one was open for 3% of the time, Pallas kernels for 10%

profile of v1, /device:TPU:0, one launch (start us, length us, event | category | flops | bytes accessed | tf_op | source)
XLA Modules:
  0.0 209.7 jit_solution(8703992660259445924)
XLA Ops:
  0.7 3.0 %collective-permute-start = (s32[8,48]{1,0:T(8,128)}, s32[8,48]{1,0:T(8,128)S(1)}, u32[]{:S(2)}, u32[]{:S(2)}) collective-permute-start(s32[8,48]{1,0:T(8,128)} %bitcast.64), channel_id=1, source_target_pairs={{0,16},{16,0},{1,17},{17,1},{2,18},{18,2},{3,19},{19,3},{4,20},{20... | collective-permute-start | bytes 4616 | tf_op jit(solution)/shard_map/ppermute | solution.py:741
  13.8 2.6 %collective-permute-start.2 = (bf16[32,1280]{1,0:T(8,128)(2,1)S(1)}, bf16[32,1280]{1,0:T(8,128)(2,1)S(1)}, u32[]{:S(2)}, u32[]{:S(2)}) collective-permute-start(bf16[32,1280]{1,0:T(8,128)(2,1)S(1)} %get-tuple-element.100), channel_id=1, source_target_pairs={{0,8},{4,12},{8,0},{12,4},{1,9},{5,13},{9,1},{13,5},{2,10},{6,14},... | collective-permute-start | bytes 245768 | tf_op jit(solution)/shard_map/ppermute | solution.py:746
  19.3 2.3 %collective-permute-done.2.refs_8_ = bf16[32,1280]{1,0:T(8,128)(2,1)S(1)} collective-permute-done((bf16[32,1280]{1,0:T(8,128)(2,1)S(1)}, bf16[32,1280]{1,0:T(8,128)(2,1)S(1)}, u32[]{:S(2)}, u32[]{:S(2)}) %collective-permute-start.2) | collective-permute-done | bytes 81952 | tf_op jit(solution)/shard_map/ppermute | solution.py:746
  33.3 3.1 %collective-permute-start.12 = (bf16[32,1280]{1,0:T(8,128)(2,1)S(1)}, bf16[32,1280]{1,0:T(8,128)(2,1)S(1)}, u32[]{:S(2)}, u32[]{:S(2)}) collective-permute-start(bf16[32,1280]{1,0:T(8,128)(2,1)S(1)} %get-tuple-element.117), channel_id=1, source_target_pairs={{0,4},{4,0},{8,12},{12,8},{1,5},{5,1},{9,13},{13,9},{2,6},{6,2},{1... | collective-permute-start | bytes 245768 | tf_op jit(solution)/shard_map/ppermute | solution.py:746
  47.7 5.3 %collective-permute-start.18 = (bf16[32,1280]{1,0:T(8,128)(2,1)}, bf16[32,1280]{1,0:T(8,128)(2,1)S(1)}, u32[]{:S(2)}, u32[]{:S(2)}) collective-permute-start(bf16[32,1280]{1,0:T(8,128)(2,1)} %get-tuple-element.137), channel_id=1, source_target_pairs={{0,4},{4,0},{8,12},{12,8},{1,5},{5,1},{9,13},{13,9},{2,6},{6,2},{1... | collective-permute-start | bytes 245768 | tf_op jit(solution)/shard_map/ppermute | solution.py:746
  53.1 2.4 %collective-permute-start.20 = (bf16[32,1280]{1,0:T(8,128)(2,1)}, bf16[32,1280]{1,0:T(8,128)(2,1)S(1)}, u32[]{:S(2)}, u32[]{:S(2)}) collective-permute-start(bf16[32,1280]{1,0:T(8,128)(2,1)} %get-tuple-element.139), channel_id=1, source_target_pairs={{0,12},{4,8},{8,4},{12,0},{1,13},{5,9},{9,5},{13,1},{2,14},{6,10},... | collective-permute-start | bytes 245768 | tf_op jit(solution)/shard_map/ppermute | solution.py:746
  61.0 2.4 %collective-permute-start.23 = (bf16[32,1280]{1,0:T(8,128)(2,1)}, bf16[32,1280]{1,0:T(8,128)(2,1)S(1)}, u32[]{:S(2)}, u32[]{:S(2)}) collective-permute-start(bf16[32,1280]{1,0:T(8,128)(2,1)} %copy-done.22), channel_id=1, source_target_pairs={{0,12},{4,8},{8,4},{12,0},{1,13},{5,9},{9,5},{13,1},{2,14},{6,10},... | collective-permute-start | bytes 245768 | tf_op jit(solution)/shard_map/ppermute | solution.py:746
  66.3 2.4 %collective-permute-start.33 = (bf16[32,1280]{1,0:T(8,128)(2,1)S(1)}, bf16[32,1280]{1,0:T(8,128)(2,1)S(1)}, u32[]{:S(2)}, u32[]{:S(2)}) collective-permute-start(bf16[32,1280]{1,0:T(8,128)(2,1)S(1)} %get-tuple-element.159), channel_id=1, source_target_pairs={{0,12},{4,8},{8,4},{12,0},{1,13},{5,9},{9,5},{13,1},{2,14},{6,10},... | collective-permute-start | bytes 245768 | tf_op jit(solution)/shard_map/ppermute | solution.py:746
  68.6 2.7 %collective-permute-done.22.refs_8_ = bf16[32,1280]{1,0:T(8,128)(2,1)S(1)} collective-permute-done((bf16[32,1280]{1,0:T(8,128)(2,1)}, bf16[32,1280]{1,0:T(8,128)(2,1)S(1)}, u32[]{:S(2)}, u32[]{:S(2)}) %collective-permute-start.22) | collective-permute-done | bytes 81952 | tf_op jit(solution)/shard_map/ppermute | solution.py:746
  72.1 2.5 %collective-permute-done.32.refs_4_ = bf16[32,1280]{1,0:T(8,128)(2,1)S(1)} collective-permute-done((bf16[32,1280]{1,0:T(8,128)(2,1)S(1)}, bf16[32,1280]{1,0:T(8,128)(2,1)S(1)}, u32[]{:S(2)}, u32[]{:S(2)}) %collective-permute-start.32) | collective-permute-done | bytes 81952 | tf_op jit(solution)/shard_map/ppermute | solution.py:746
  77.8 3.2 %collective-permute-start.24 = (bf16[32,1280]{1,0:T(8,128)(2,1)S(1)}, bf16[32,1280]{1,0:T(8,128)(2,1)S(1)}, u32[]{:S(2)}, u32[]{:S(2)}) collective-permute-start(bf16[32,1280]{1,0:T(8,128)(2,1)S(1)} %get-tuple-element.151), channel_id=1, source_target_pairs={{0,4},{4,0},{8,12},{12,8},{1,5},{5,1},{9,13},{13,9},{2,6},{6,2},{1... | collective-permute-start | bytes 245768 | tf_op jit(solution)/shard_map/ppermute | solution.py:746
  83.5 2.4 %copy-done.2 = bf16[1280,2000]{0,1:T(8,128)(2,1)S(1)} copy-done((bf16[1280,2000]{0,1:T(8,128)(2,1)S(1)}, bf16[1280,2000]{0,1:T(8,128)(2,1)}, u32[]{:S(2)}) %copy-start.2) | copy-done | bytes 5120024
  87.9 3.5 %collective-permute-done.25.refs_4_ = bf16[32,1280]{1,0:T(8,128)(2,1)S(1)} collective-permute-done((bf16[32,1280]{1,0:T(8,128)(2,1)S(1)}, bf16[32,1280]{1,0:T(8,128)(2,1)S(1)}, u32[]{:S(2)}, u32[]{:S(2)}) %collective-permute-start.25) | collective-permute-done | bytes 81952 | tf_op jit(solution)/shard_map/ppermute | solution.py:746
  92.9 4.5 %collective-permute-start.27 = (bf16[96,1280]{1,0:T(8,128)(2,1)S(1)}, bf16[96,1280]{1,0:T(8,128)(2,1)S(1)}, u32[]{:S(2)}, u32[]{:S(2)}) collective-permute-start(bf16[96,1280]{1,0:T(8,128)(2,1)S(1)} %shard_map.141.refs_0_), channel_id=1, source_target_pairs={{0,4},{4,0},{8,12},{12,8},{1,5},{5,1},{9,13},{13,9},{2,6},{6,2},{1... | collective-permute-start | bytes 737288 | tf_op jit(solution)/shard_map/ppermute | solution.py:746
  100.6 2.5 %collective-permute-done.27.refs_1_ = bf16[96,1280]{1,0:T(8,128)(2,1)S(1)} collective-permute-done((bf16[96,1280]{1,0:T(8,128)(2,1)S(1)}, bf16[96,1280]{1,0:T(8,128)(2,1)S(1)}, u32[]{:S(2)}, u32[]{:S(2)}) %collective-permute-start.27) | collective-permute-done | bytes 245792 | tf_op jit(solution)/shard_map/ppermute | solution.py:746
  105.1 3.7 %collective-permute-done.36.refs_3_ = bf16[96,1280]{1,0:T(8,128)(2,1)S(1)} collective-permute-done((bf16[96,1280]{1,0:T(8,128)(2,1)S(1)}, bf16[96,1280]{1,0:T(8,128)(2,1)S(1)}, u32[]{:S(2)}, u32[]{:S(2)}) %collective-permute-start.36) | collective-permute-done | bytes 245792 | tf_op jit(solution)/shard_map/ppermute | solution.py:1069
  108.8 5.3 %collective-permute-done.38.refs_5_ = bf16[96,1280]{1,0:T(8,128)(2,1)S(1)} collective-permute-done((bf16[96,1280]{1,0:T(8,128)(2,1)S(1)}, bf16[96,1280]{1,0:T(8,128)(2,1)S(1)}, u32[]{:S(2)}, u32[]{:S(2)}) %collective-permute-start.38) | collective-permute-done | bytes 245792 | tf_op jit(solution)/shard_map/ppermute | solution.py:1072
  114.1 3.2 %shard_map.143 = (f32[2048,384]{1,0:T(8,128)S(1)}, bf16[384,1280]{1,0:T(8,128)(2,1)S(1)}, f32[4,16,96]{2,1,0:T(8,128)S(1)}) custom-call(s32[1]{0:T(128)} %bitcast.28.member_ref, bf16[2000,1280]{1,0:T(8,128)(2,1)S(1)} %bitcast.58, bf16[256,1280]{1,0:T(8,128)(2,1)S(1)} %get-tuple-element.121.label_ref, bf16[96,1280]{1,0:T(8,128)(2,1)S(1)} %shard_map.142.refs_0_, ...), custom_call_target="tpu_custom_call" | custom-call | flops 2013265920 | tf_op jit(solution)/shard_map/pallas_call | solution.py:441
  118.7 6.8 %collective-permute-done.39.refs_5_ = bf16[96,1280]{1,0:T(8,128)(2,1)S(1)} collective-permute-done((bf16[96,1280]{1,0:T(8,128)(2,1)S(1)}, bf16[96,1280]{1,0:T(8,128)(2,1)S(1)}, u32[]{:S(2)}, u32[]{:S(2)}) %collective-permute-start.39) | collective-permute-done | bytes 245792 | tf_op jit(solution)/shard_map/ppermute | solution.py:1072
  125.5 3.2 %shard_map.144 = (f32[2048,384]{1,0:T(8,128)S(1)}, bf16[384,1280]{1,0:T(8,128)(2,1)S(1)}, f32[8,16,96]{2,1,0:T(8,128)S(1)}) custom-call(s32[1]{0:T(128)} %bitcast.28.member_ref, bf16[2000,1280]{1,0:T(8,128)(2,1)S(1)} %bitcast.59, bf16[256,1280]{1,0:T(8,128)(2,1)S(1)} %get-tuple-element.121.label_ref, bf16[96,1280]{1,0:T(8,128)(2,1)S(1)} %shard_map.141.refs_0_, ...), custom_call_target="tpu_custom_call" | custom-call | flops 2013265920 | tf_op jit(solution)/shard_map/pallas_call | solution.py:441
  130.1 2.9 %collective-permute-done.40.refs_1_ = f32[8,16,96]{2,1,0:T(8,128)S(1)} collective-permute-done((f32[8,16,96]{2,1,0:T(8,128)S(1)}, f32[8,16,96]{2,1,0:T(8,128)S(1)}, u32[]{:S(2)}, u32[]{:S(2)}) %collective-permute-start.40) | collective-permute-done | bytes 49184 | tf_op jit(solution)/shard_map/ppermute | solution.py:746
  134.0 4.3 %collective-permute-done.42.refs_3_ = f32[8,16,96]{2,1,0:T(8,128)S(1)} collective-permute-done((f32[8,16,96]{2,1,0:T(8,128)S(1)}, f32[8,16,96]{2,1,0:T(8,128)S(1)}, u32[]{:S(2)}, u32[]{:S(2)}) %collective-permute-start.42) | collective-permute-done | bytes 49184 | tf_op jit(solution)/shard_map/ppermute | solution.py:746
  138.3 7.1 %shard_map.145 = (f32[16,768]{1,0:T(8,128)S(1)}, bf16[256,768]{1,0:T(8,128)(2,1)S(1)}, bf16[256,768]{1,0:T(8,128)(2,1)S(1)}, f32[1,4]{1,0:T(1,128)}) custom-call(s32[32]{0:T(128)S(1)} %copy-done.19, s32[16,128]{1,0:T(8,128)S(1)} %get-tuple-element.120.notes_ref, f32[8,16,96]{2,1,0:T(8,128)S(1)} %get-tuple-element.164.refs_0_, ...), custom_call_target="tpu_custom_call" | custom-call | flops 67108864 | tf_op jit(solution)/shard_map/pallas_call | solution.py:632
  145.5 4.9 %shard_map.146 = (bf16[512,1280]{1,0:T(8,128)(2,1)S(1)}, bf16[512,1280]{1,0:T(8,128)(2,1)S(1)}) custom-call(s32[4]{0:T(128)S(1)} %copy-done.20, f32[2048,384]{1,0:T(8,128)S(1)} %get-tuple-element.171.refs_0_, f32[2048,384]{1,0:T(8,128)S(1)} %get-tuple-element.172.refs_1_, bf16[384,1280]{1,0:T(8,128)(2,1)S(1)} %get-tuple-element.173.refs_2_, ...), custom_call_target="tpu_custom_call" | custom-call | flops 2818572288 | tf_op jit(solution)/shard_map/pallas_call | solution.py:683
  151.0 2.8 %shard_map.147.own_ref = bf16[512,1280]{1,0:T(8,128)(2,1)S(1)} custom-call(s32[2]{0:T(128)S(1)} %get-tuple-element.180.order_ref, f32[2048,384]{1,0:T(8,128)S(1)} %get-tuple-element.171.refs_0_, f32[2048,384]{1,0:T(8,128)S(1)} %get-tuple-element.172.refs_1_, bf16[384,1280]{1,0:T(8,128)(2,1)S(1)} %get-tuple-element.173.refs_2_, ...), custom_call_target="tpu_custom_call" | custom-call | flops 1409286144 | tf_op jit(solution)/shard_map/pallas_call | solution.py:683
  158.8 2.8 %shard_map.149.own_ref = bf16[512,1280]{1,0:T(8,128)(2,1)S(1)} custom-call(s32[2]{0:T(128)S(1)} %get-tuple-element.182.order_ref, f32[2048,384]{1,0:T(8,128)S(1)} %get-tuple-element.171.refs_0_, f32[2048,384]{1,0:T(8,128)S(1)} %get-tuple-element.172.refs_1_, bf16[384,1280]{1,0:T(8,128)(2,1)S(1)} %get-tuple-element.173.refs_2_, ...), custom_call_target="tpu_custom_call" | custom-call | flops 1409286144 | tf_op jit(solution)/shard_map/pallas_call | solution.py:683
  161.6 3.7 %collective-permute-done.46.refs_0_ = bf16[128,1280]{1,0:T(8,128)(2,1)S(1)} collective-permute-done((bf16[128,1280]{1,0:T(8,128)(2,1)S(1)}, bf16[128,1280]{1,0:T(8,128)(2,1)S(1)}, u32[]{:S(2)}, u32[]{:S(2)}) %collective-permute-start.46) | collective-permute-done | bytes 327712 | tf_op jit(solution)/shard_map/ppermute | solution.py:741
  169.7 2.6 %collective-permute-done.45.refs_0_ = bf16[128,1280]{1,0:T(8,128)(2,1)S(1)} collective-permute-done((bf16[128,1280]{1,0:T(8,128)(2,1)S(1)}, bf16[128,1280]{1,0:T(8,128)(2,1)S(1)}, u32[]{:S(2)}, u32[]{:S(2)}) %collective-permute-start.45) | collective-permute-done | bytes 327712 | tf_op jit(solution)/shard_map/ppermute | solution.py:741
  173.1 5.8 %collective-permute-done.48.refs_1_ = bf16[128,1280]{1,0:T(8,128)(2,1)S(1)} collective-permute-done((bf16[128,1280]{1,0:T(8,128)(2,1)S(1)}, bf16[128,1280]{1,0:T(8,128)(2,1)S(1)}, u32[]{:S(2)}, u32[]{:S(2)}) %collective-permute-start.48) | collective-permute-done | bytes 327712 | tf_op jit(solution)/shard_map/ppermute | solution.py:741
  183.9 6.6 %collective-permute-done.53.refs_2_ = bf16[128,1280]{1,0:T(8,128)(2,1)S(1)} collective-permute-done((bf16[128,1280]{1,0:T(8,128)(2,1)S(1)}, bf16[128,1280]{1,0:T(8,128)(2,1)S(1)}, u32[]{:S(2)}, u32[]{:S(2)}) %collective-permute-start.53) | collective-permute-done | bytes 327712 | tf_op jit(solution)/shard_map/ppermute | solution.py:741
  193.3 4.2 %collective-permute-done.51.refs_0_ = bf16[128,1280]{1,0:T(8,128)(2,1)S(1)} collective-permute-done((bf16[128,1280]{1,0:T(8,128)(2,1)S(1)}, bf16[128,1280]{1,0:T(8,128)(2,1)S(1)}, u32[]{:S(2)}, u32[]{:S(2)}) %collective-permute-start.51) | collective-permute-done | bytes 327712 | tf_op jit(solution)/shard_map/ppermute | solution.py:741
  199.1 4.6 %collective-permute-done.54.refs_2_ = bf16[128,1280]{1,0:T(8,128)(2,1)S(1)} collective-permute-done((bf16[128,1280]{1,0:T(8,128)(2,1)S(1)}, bf16[128,1280]{1,0:T(8,128)(2,1)S(1)}, u32[]{:S(2)}, u32[]{:S(2)}) %collective-permute-start.54) | collective-permute-done | bytes 327712 | tf_op jit(solution)/shard_map/ppermute | solution.py:741
  (199 shorter events, 88.9 us)
Async XLA Ops:
  9.1 20.6 %collective-permute-start.8 = (bf16[1280,128]{1,0:T(8,128)(2,1)S(1)}, bf16[1280,128]{1,0:T(8,128)(2,1)S(1)}, u32[]{:S(2)}, u32[]{:S(2)}) collective-permute-start(bf16[1280,128]{1,0:T(8,128)(2,1)S(1)} %get-tuple-element.108), channel_id=1, source_target_pairs={{0,16},{16,0},{1,17},{17,1},{2,18},{18,2},{3,19},{19,3},{4,20},{20... | collective-permute-start | bytes 983048 | tf_op jit(solution)/shard_map/ppermute | solution.py:741
  9.8 19.9 %collective-permute-start.9 = (bf16[128,1280]{1,0:T(8,128)(2,1)S(1)}, bf16[128,1280]{1,0:T(8,128)(2,1)S(1)}, u32[]{:S(2)}, u32[]{:S(2)}) collective-permute-start(bf16[128,1280]{1,0:T(8,128)(2,1)S(1)} %get-tuple-element.109), channel_id=1, source_target_pairs={{0,16},{16,0},{1,17},{17,1},{2,18},{18,2},{3,19},{19,3},{4,20},{20... | collective-permute-start | bytes 983048 | tf_op jit(solution)/shard_map/ppermute | solution.py:741
  39.5 13.5 %collective-permute-start.15 = (bf16[32,1280]{1,0:T(8,128)(2,1)S(1)}, bf16[32,1280]{1,0:T(8,128)(2,1)S(1)}, u32[]{:S(2)}, u32[]{:S(2)}) collective-permute-start(bf16[32,1280]{1,0:T(8,128)(2,1)S(1)} %get-tuple-element.129), channel_id=1, source_target_pairs={{0,4},{4,0},{8,12},{12,8},{1,5},{5,1},{9,13},{13,9},{2,6},{6,2},{1... | collective-permute-start | bytes 245768 | tf_op jit(solution)/shard_map/ppermute | solution.py:746
  40.7 14.8 %collective-permute-start.16 = (bf16[32,1280]{1,0:T(8,128)(2,1)S(1)}, bf16[32,1280]{1,0:T(8,128)(2,1)S(1)}, u32[]{:S(2)}, u32[]{:S(2)}) collective-permute-start(bf16[32,1280]{1,0:T(8,128)(2,1)S(1)} %get-tuple-element.130), channel_id=1, source_target_pairs={{0,8},{4,12},{8,0},{12,4},{1,9},{5,13},{9,1},{13,5},{2,10},{6,14},... | collective-permute-start | bytes 245768 | tf_op jit(solution)/shard_map/ppermute | solution.py:746
  42.0 13.5 %collective-permute-start.17 = (bf16[32,1280]{1,0:T(8,128)(2,1)S(1)}, bf16[32,1280]{1,0:T(8,128)(2,1)S(1)}, u32[]{:S(2)}, u32[]{:S(2)}) collective-permute-start(bf16[32,1280]{1,0:T(8,128)(2,1)S(1)} %get-tuple-element.131), channel_id=1, source_target_pairs={{0,12},{4,8},{8,4},{12,0},{1,13},{5,9},{9,5},{13,1},{2,14},{6,10},... | collective-permute-start | bytes 245768 | tf_op jit(solution)/shard_map/ppermute | solution.py:746
  47.7 13.3 %collective-permute-start.18 = (bf16[32,1280]{1,0:T(8,128)(2,1)}, bf16[32,1280]{1,0:T(8,128)(2,1)S(1)}, u32[]{:S(2)}, u32[]{:S(2)}) collective-permute-start(bf16[32,1280]{1,0:T(8,128)(2,1)} %get-tuple-element.137), channel_id=1, source_target_pairs={{0,4},{4,0},{8,12},{12,8},{1,5},{5,1},{9,13},{13,9},{2,6},{6,2},{1... | collective-permute-start | bytes 245768 | tf_op jit(solution)/shard_map/ppermute | solution.py:746
  53.1 10.3 %collective-permute-start.19 = (bf16[32,1280]{1,0:T(8,128)(2,1)}, bf16[32,1280]{1,0:T(8,128)(2,1)S(1)}, u32[]{:S(2)}, u32[]{:S(2)}) collective-permute-start(bf16[32,1280]{1,0:T(8,128)(2,1)} %get-tuple-element.138), channel_id=1, source_target_pairs={{0,8},{4,12},{8,0},{12,4},{1,9},{5,13},{9,1},{13,5},{2,10},{6,14},... | collective-permute-start | bytes 245768 | tf_op jit(solution)/shard_map/ppermute | solution.py:746
  53.1 10.3 %collective-permute-start.20 = (bf16[32,1280]{1,0:T(8,128)(2,1)}, bf16[32,1280]{1,0:T(8,128)(2,1)S(1)}, u32[]{:S(2)}, u32[]{:S(2)}) collective-permute-start(bf16[32,1280]{1,0:T(8,128)(2,1)} %get-tuple-element.139), channel_id=1, source_target_pairs={{0,12},{4,8},{8,4},{12,0},{1,13},{5,9},{9,5},{13,1},{2,14},{6,10},... | collective-permute-start | bytes 245768 | tf_op jit(solution)/shard_map/ppermute | solution.py:746
  60.1 11.2 %collective-permute-start.22 = (bf16[32,1280]{1,0:T(8,128)(2,1)}, bf16[32,1280]{1,0:T(8,128)(2,1)S(1)}, u32[]{:S(2)}, u32[]{:S(2)}) collective-permute-start(bf16[32,1280]{1,0:T(8,128)(2,1)} %copy-done.23), channel_id=1, source_target_pairs={{0,8},{4,12},{8,0},{12,4},{1,9},{5,13},{9,1},{13,5},{2,10},{6,14},... | collective-permute-start | bytes 245768 | tf_op jit(solution)/shard_map/ppermute | solution.py:746
  61.0 10.3 %collective-permute-start.23 = (bf16[32,1280]{1,0:T(8,128)(2,1)}, bf16[32,1280]{1,0:T(8,128)(2,1)S(1)}, u32[]{:S(2)}, u32[]{:S(2)}) collective-permute-start(bf16[32,1280]{1,0:T(8,128)(2,1)} %copy-done.22), channel_id=1, source_target_pairs={{0,12},{4,8},{8,4},{12,0},{1,13},{5,9},{9,5},{13,1},{2,14},{6,10},... | collective-permute-start | bytes 245768 | tf_op jit(solution)/shard_map/ppermute | solution.py:746
  75.5 16.7 %collective-permute-start.34 = (bf16[96,1280]{1,0:T(8,128)(2,1)S(1)}, bf16[96,1280]{1,0:T(8,128)(2,1)S(1)}, u32[]{:S(2)}, u32[]{:S(2)}) collective-permute-start(bf16[96,1280]{1,0:T(8,128)(2,1)S(1)} %shard_map.142.refs_0_), channel_id=1, source_target_pairs={{0,4},{4,0},{8,12},{12,8},{1,5},{5,1},{9,13},{13,9},{2,6},{6,2},{1... | collective-permute-start | bytes 737288 | tf_op jit(solution)/shard_map/ppermute | solution.py:746
  77.0 15.2 %collective-permute-start.35 = (bf16[96,1280]{1,0:T(8,128)(2,1)S(1)}, bf16[96,1280]{1,0:T(8,128)(2,1)S(1)}, u32[]{:S(2)}, u32[]{:S(2)}) collective-permute-start(bf16[96,1280]{1,0:T(8,128)(2,1)S(1)} %shard_map.142.refs_0_), channel_id=1, source_target_pairs={{4,8},{8,4},{5,9},{9,5},{6,10},{10,6},{7,11},{11,7},{20,24},{24,20... | collective-permute-start | bytes 737288 | tf_op jit(solution)/shard_map/ppermute | solution.py:1066
  81.1 10.3 %collective-permute-start.25 = (bf16[32,1280]{1,0:T(8,128)(2,1)S(1)}, bf16[32,1280]{1,0:T(8,128)(2,1)S(1)}, u32[]{:S(2)}, u32[]{:S(2)}) collective-permute-start(bf16[32,1280]{1,0:T(8,128)(2,1)S(1)} %get-tuple-element.152), channel_id=1, source_target_pairs={{0,8},{4,12},{8,0},{12,4},{1,9},{5,13},{9,1},{13,5},{2,10},{6,14},... | collective-permute-start | bytes 245768 | tf_op jit(solution)/shard_map/ppermute | solution.py:746
  92.9 10.2 %collective-permute-start.27 = (bf16[96,1280]{1,0:T(8,128)(2,1)S(1)}, bf16[96,1280]{1,0:T(8,128)(2,1)S(1)}, u32[]{:S(2)}, u32[]{:S(2)}) collective-permute-start(bf16[96,1280]{1,0:T(8,128)(2,1)S(1)} %shard_map.141.refs_0_), channel_id=1, source_target_pairs={{0,4},{4,0},{8,12},{12,8},{1,5},{5,1},{9,13},{13,9},{2,6},{6,2},{1... | collective-permute-start | bytes 737288 | tf_op jit(solution)/shard_map/ppermute | solution.py:746
  98.0 10.8 %collective-permute-start.36 = (bf16[96,1280]{1,0:T(8,128)(2,1)S(1)}, bf16[96,1280]{1,0:T(8,128)(2,1)S(1)}, u32[]{:S(2)}, u32[]{:S(2)}) collective-permute-start(bf16[96,1280]{1,0:T(8,128)(2,1)S(1)} %collective-permute-done.35.refs_2_), channel_id=1, source_target_pairs={{4,0},{8,12},{5,1},{9,13},{6,2},{10,14},{7,3},{11,15},{20,16},{24,... | collective-permute-start | bytes 737288 | tf_op jit(solution)/shard_map/ppermute | solution.py:1069
  99.3 14.7 %collective-permute-start.38 = (bf16[96,1280]{1,0:T(8,128)(2,1)S(1)}, bf16[96,1280]{1,0:T(8,128)(2,1)S(1)}, u32[]{:S(2)}, u32[]{:S(2)}) collective-permute-start(bf16[96,1280]{1,0:T(8,128)(2,1)S(1)} %collective-permute-done.37.refs_4_), channel_id=1, source_target_pairs={{4,0},{8,12},{5,1},{9,13},{6,2},{10,14},{7,3},{11,15},{20,16},{24,... | collective-permute-start | bytes 737288 | tf_op jit(solution)/shard_map/ppermute | solution.py:1072
  103.1 14.2 %collective-permute-start.30 = (bf16[96,1280]{1,0:T(8,128)(2,1)S(1)}, bf16[96,1280]{1,0:T(8,128)(2,1)S(1)}, u32[]{:S(2)}, u32[]{:S(2)}) collective-permute-start(bf16[96,1280]{1,0:T(8,128)(2,1)S(1)} %collective-permute-done.27.refs_1_), channel_id=1, source_target_pairs={{4,8},{8,4},{5,9},{9,5},{6,10},{10,6},{7,11},{11,7},{20,24},{24,20... | collective-permute-start | bytes 737288 | tf_op jit(solution)/shard_map/ppermute | solution.py:1068
  103.8 14.9 %collective-permute-start.29 = (bf16[96,1280]{1,0:T(8,128)(2,1)S(1)}, bf16[96,1280]{1,0:T(8,128)(2,1)S(1)}, u32[]{:S(2)}, u32[]{:S(2)}) collective-permute-start(bf16[96,1280]{1,0:T(8,128)(2,1)S(1)} %collective-permute-done.28.refs_2_), channel_id=1, source_target_pairs={{4,0},{8,12},{5,1},{9,13},{6,2},{10,14},{7,3},{11,15},{20,16},{24,... | collective-permute-start | bytes 737288 | tf_op jit(solution)/shard_map/ppermute | solution.py:1069
  150.5 11.2 %collective-permute-start.44 = (bf16[512,1280]{1,0:T(8,128)(2,1)S(1)}, bf16[512,1280]{1,0:T(8,128)(2,1)S(1)}, u32[]{:S(2)}, u32[]{:S(2)}) collective-permute-start(bf16[512,1280]{1,0:T(8,128)(2,1)S(1)} %get-tuple-element.183), channel_id=1, source_target_pairs={{0,1},{1,0},{2,3},{3,2},{4,5},{5,4},{6,7},{7,6},{8,9},{9,8},{10,11... | collective-permute-start | bytes 3932168 | tf_op jit(solution)/shard_map/ppermute | solution.py:741
  154.7 10.6 %collective-permute-start.46 = (bf16[128,1280]{1,0:T(8,128)(2,1)S(1)}, bf16[128,1280]{1,0:T(8,128)(2,1)S(1)}, u32[]{:S(2)}, u32[]{:S(2)}) collective-permute-start(bf16[128,1280]{1,0:T(8,128)(2,1)S(1)} %get-tuple-element.181), channel_id=1, source_target_pairs={{0,16},{16,0},{1,17},{17,1},{2,18},{18,2},{3,19},{19,3},{4,20},{20... | collective-permute-start | bytes 983048 | tf_op jit(solution)/shard_map/ppermute | solution.py:741
  155.5 10.6 %collective-permute-start.47 = (bf16[128,1280]{1,0:T(8,128)(2,1)S(1)}, bf16[128,1280]{1,0:T(8,128)(2,1)S(1)}, u32[]{:S(2)}, u32[]{:S(2)}) collective-permute-start(bf16[128,1280]{1,0:T(8,128)(2,1)S(1)} %get-tuple-element.185), channel_id=1, source_target_pairs={{0,2},{2,0},{1,3},{3,1},{4,6},{6,4},{5,7},{7,5},{8,10},{10,8},{9,1... | collective-permute-start | bytes 983048 | tf_op jit(solution)/shard_map/ppermute | solution.py:741
  157.0 15.3 %collective-permute-start.45 = (bf16[128,1280]{1,0:T(8,128)(2,1)S(1)}, bf16[128,1280]{1,0:T(8,128)(2,1)S(1)}, u32[]{:S(2)}, u32[]{:S(2)}) collective-permute-start(bf16[128,1280]{1,0:T(8,128)(2,1)S(1)} %get-tuple-element.184), channel_id=1, source_target_pairs={{0,16},{16,0},{1,17},{17,1},{2,18},{18,2},{3,19},{19,3},{4,20},{20... | collective-permute-start | bytes 983048 | tf_op jit(solution)/shard_map/ppermute | solution.py:741
  158.3 14.8 %collective-permute-start.49 = (bf16[128,1280]{1,0:T(8,128)(2,1)S(1)}, bf16[128,1280]{1,0:T(8,128)(2,1)S(1)}, u32[]{:S(2)}, u32[]{:S(2)}) collective-permute-start(bf16[128,1280]{1,0:T(8,128)(2,1)S(1)} %get-tuple-element.187), channel_id=1, source_target_pairs={{0,2},{2,0},{1,3},{3,1},{4,6},{6,4},{5,7},{7,5},{8,10},{10,8},{9,1... | collective-permute-start | bytes 983048 | tf_op jit(solution)/shard_map/ppermute | solution.py:741
  166.9 12.1 %collective-permute-start.48 = (bf16[128,1280]{1,0:T(8,128)(2,1)S(1)}, bf16[128,1280]{1,0:T(8,128)(2,1)S(1)}, u32[]{:S(2)}, u32[]{:S(2)}) collective-permute-start(bf16[128,1280]{1,0:T(8,128)(2,1)S(1)} %get-tuple-element.186), channel_id=1, source_target_pairs={{0,2},{2,0},{1,3},{3,1},{4,6},{6,4},{5,7},{7,5},{8,10},{10,8},{9,1... | collective-permute-start | bytes 983048 | tf_op jit(solution)/shard_map/ppermute | solution.py:741
  168.4 10.5 %collective-permute-start.50 = (bf16[128,1280]{1,0:T(8,128)(2,1)S(1)}, bf16[128,1280]{1,0:T(8,128)(2,1)S(1)}, u32[]{:S(2)}, u32[]{:S(2)}) collective-permute-start(bf16[128,1280]{1,0:T(8,128)(2,1)S(1)} %get-tuple-element.188), channel_id=1, source_target_pairs={{0,16},{16,0},{1,17},{17,1},{2,18},{18,2},{3,19},{19,3},{4,20},{20... | collective-permute-start | bytes 983048 | tf_op jit(solution)/shard_map/ppermute | solution.py:741
  179.8 10.7 %collective-permute-start.53 = (bf16[128,1280]{1,0:T(8,128)(2,1)S(1)}, bf16[128,1280]{1,0:T(8,128)(2,1)S(1)}, u32[]{:S(2)}, u32[]{:S(2)}) collective-permute-start(bf16[128,1280]{1,0:T(8,128)(2,1)S(1)} %get-tuple-element.190.refs_0_), channel_id=1, source_target_pairs={{0,2},{2,0},{1,3},{3,1},{4,6},{6,4},{5,7},{7,5},{8,10},{10,8},{9,1... | collective-permute-start | bytes 983048 | tf_op jit(solution)/shard_map/ppermute | solution.py:741
  181.4 10.6 %collective-permute-start.55 = (bf16[128,1280]{1,0:T(8,128)(2,1)S(1)}, bf16[128,1280]{1,0:T(8,128)(2,1)S(1)}, u32[]{:S(2)}, u32[]{:S(2)}) collective-permute-start(bf16[128,1280]{1,0:T(8,128)(2,1)S(1)} %get-tuple-element.189.refs_1_), channel_id=1, source_target_pairs={{0,16},{16,0},{1,17},{17,1},{2,18},{18,2},{3,19},{19,3},{4,20},{20... | collective-permute-start | bytes 983048 | tf_op jit(solution)/shard_map/ppermute | solution.py:741
  182.7 14.9 %collective-permute-start.51 = (bf16[128,1280]{1,0:T(8,128)(2,1)S(1)}, bf16[128,1280]{1,0:T(8,128)(2,1)S(1)}, u32[]{:S(2)}, u32[]{:S(2)}) collective-permute-start(bf16[128,1280]{1,0:T(8,128)(2,1)S(1)} %get-tuple-element.189.refs_1_), channel_id=1, source_target_pairs={{0,2},{2,0},{1,3},{3,1},{4,6},{6,4},{5,7},{7,5},{8,10},{10,8},{9,1... | collective-permute-start | bytes 983048 | tf_op jit(solution)/shard_map/ppermute | solution.py:741
  183.2 15.9 %collective-permute-start.52 = (bf16[128,1280]{1,0:T(8,128)(2,1)S(1)}, bf16[128,1280]{1,0:T(8,128)(2,1)S(1)}, u32[]{:S(2)}, u32[]{:S(2)}) collective-permute-start(bf16[128,1280]{1,0:T(8,128)(2,1)S(1)} %get-tuple-element.190.refs_0_), channel_id=1, source_target_pairs={{0,16},{16,0},{1,17},{17,1},{2,18},{18,2},{3,19},{19,3},{4,20},{20... | collective-permute-start | bytes 983048 | tf_op jit(solution)/shard_map/ppermute | solution.py:741
  190.5 13.2 %collective-permute-start.54 = (bf16[128,1280]{1,0:T(8,128)(2,1)S(1)}, bf16[128,1280]{1,0:T(8,128)(2,1)S(1)}, u32[]{:S(2)}, u32[]{:S(2)}) collective-permute-start(bf16[128,1280]{1,0:T(8,128)(2,1)S(1)} %collective-permute-done.53.refs_2_), channel_id=1, source_target_pairs={{0,16},{16,0},{1,17},{17,1},{2,18},{18,2},{3,19},{19,3},{4,20},{20... | collective-permute-start | bytes 983048 | tf_op jit(solution)/shard_map/ppermute | solution.py:741
  192.0 11.7 %collective-permute-start.56 = (bf16[128,1280]{1,0:T(8,128)(2,1)S(1)}, bf16[128,1280]{1,0:T(8,128)(2,1)S(1)}, u32[]{:S(2)}, u32[]{:S(2)}) collective-permute-start(bf16[128,1280]{1,0:T(8,128)(2,1)S(1)} %collective-permute-done.55.refs_3_), channel_id=1, source_target_pairs={{0,2},{2,0},{1,3},{3,1},{4,6},{6,4},{5,7},{7,5},{8,10},{10,8},{9,1... | collective-permute-start | bytes 983048 | tf_op jit(solution)/shard_map/ppermute | solution.py:741
  193.3 10.9 %collective-permute-start.61 = (bf16[128,1280]{1,0:T(8,128)(2,1)S(1)}, bf16[128,1280]{1,0:T(8,128)(2,1)S(1)}, u32[]{:S(2)}, u32[]{:S(2)}) collective-permute-start(bf16[128,1280]{1,0:T(8,128)(2,1)S(1)} %get-tuple-element.190.refs_0_), channel_id=1, source_target_pairs={{0,1},{1,0},{2,3},{3,2},{4,5},{5,4},{6,7},{7,6},{8,9},{9,8},{10,11... | collective-permute-start | bytes 983048 | tf_op jit(solution)/shard_map/ppermute | solution.py:741
  (63 other events, 551.4 us)

commit v2 on v0

--- a/solution.py
+++ b/solution.py
@@ -588,7 +588,7 @@
         blank_bwd[frame_count - 1] = ends_blank
         label_bwd[frame_count - 1] = ends_label
         fwd_blank, fwd_label, _, _ = lax.fori_loop(
-            1, frame_count, advance, (first_blank, first_label, ends_blank, ends_label), unroll=4
+            1, frame_count, advance, (first_blank, first_label, ends_blank, ends_label), unroll=frame_count - 1
         )
         end_state = jnp.sum(jnp.where(lane == counts, fwd_blank, 0.0), axis=1, keepdims=True)
         near_state = jnp.sum(jnp.where(lane == counts - 1, fwd_label, 0.0), axis=1, keepdims=True)

time: 209 us -> 209 us (level)
  no operation moved by 1% of the time
where the time goes in v2:
time: 209 us
  starting transfers between devices  79.7 us (38%)
  waiting for transfers between devices  75 us (36%)
  Pallas kernels  42.5 us (20%)
  local copies, waits for them, and re-layouts  7.77 us (4%)
  other arithmetic  2.29 us (1%)
    ppermute x29, starting transfers between devices, crossed(): return lax.ppermute(value, axis, [(i, i ^ by) for i in range(count)])  48.3 us
    ppermute x28, waiting for transfers between devices, swap(): return lax.ppermute(value, axis, [(0, 1), (1, 0)])  30.9 us
    ppermute x29, waiting for transfers between devices, crossed(): return lax.ppermute(value, axis, [(i, i ^ by) for i in range(count)])  28.5 us
    ppermute x28, starting transfers between devices, swap(): return lax.ppermute(value, axis, [(0, 1), (1, 0)])  23.4 us
    ppermute x2, waiting for transfers between devices, per_device(): last = lax.ppermute(far, 'expert', OUTWARD)  12 us
    pallas_call x3, Pallas kernels, head_gradient(): call(kernel, tuple((bf16_rows(each * BLOCK_ROWS, width) for _ in range(ou...  10.6 us
    pallas_call x1, Pallas kernels, ctc_pass(): call(kernel, (jax.ShapeDtypeStruct((COLS, row_count), jnp.float32), bf16_...  6.86 us
    pallas_call x2, Pallas kernels, head_logits(): call(kernel, (jax.ShapeDtypeStruct((height, row_count), jnp.float32), bf1...  6.4 us
  transfers between devices with their start and end apart: 65, of which 29 were waited for; matrix products, arithmetic and copies ran while one was open for 2% of the time, Pallas kernels for 10%

profile of v2, /device:TPU:0, one launch (start us, length us, event | category | flops | bytes accessed | tf_op | source)
XLA Modules:
  0.0 208.8 jit_solution(10568616290431156223)
XLA Ops:
  0.7 3.0 %collective-permute-start = (s32[8,48]{1,0:T(8,128)}, s32[8,48]{1,0:T(8,128)S(1)}, u32[]{:S(2)}, u32[]{:S(2)}) collective-permute-start(s32[8,48]{1,0:T(8,128)} %bitcast.64), channel_id=1, source_target_pairs={{0,16},{16,0},{1,17},{17,1},{2,18},{18,2},{3,19},{19,3},{4,20},{20... | collective-permute-start | bytes 4616 | tf_op jit(solution)/shard_map/ppermute | solution.py:741
  11.6 2.6 %collective-permute-start.2 = (bf16[32,1280]{1,0:T(8,128)(2,1)S(1)}, bf16[32,1280]{1,0:T(8,128)(2,1)S(1)}, u32[]{:S(2)}, u32[]{:S(2)}) collective-permute-start(bf16[32,1280]{1,0:T(8,128)(2,1)S(1)} %get-tuple-element.100), channel_id=1, source_target_pairs={{0,8},{4,12},{8,0},{12,4},{1,9},{5,13},{9,1},{13,5},{2,10},{6,14},... | collective-permute-start | bytes 245768 | tf_op jit(solution)/shard_map/ppermute | solution.py:746
  37.2 2.4 %collective-permute-start.16 = (bf16[32,1280]{1,0:T(8,128)(2,1)S(1)}, bf16[32,1280]{1,0:T(8,128)(2,1)S(1)}, u32[]{:S(2)}, u32[]{:S(2)}) collective-permute-start(bf16[32,1280]{1,0:T(8,128)(2,1)S(1)} %get-tuple-element.130), channel_id=1, source_target_pairs={{0,8},{4,12},{8,0},{12,4},{1,9},{5,13},{9,1},{13,5},{2,10},{6,14},... | collective-permute-start | bytes 245768 | tf_op jit(solution)/shard_map/ppermute | solution.py:746
  45.0 5.5 %collective-permute-start.18 = (bf16[32,1280]{1,0:T(8,128)(2,1)}, bf16[32,1280]{1,0:T(8,128)(2,1)S(1)}, u32[]{:S(2)}, u32[]{:S(2)}) collective-permute-start(bf16[32,1280]{1,0:T(8,128)(2,1)} %get-tuple-element.137), channel_id=1, source_target_pairs={{0,4},{4,0},{8,12},{12,8},{1,5},{5,1},{9,13},{13,9},{2,6},{6,2},{1... | collective-permute-start | bytes 245768 | tf_op jit(solution)/shard_map/ppermute | solution.py:746
  66.1 2.3 %collective-permute-done.22.refs_8_ = bf16[32,1280]{1,0:T(8,128)(2,1)S(1)} collective-permute-done((bf16[32,1280]{1,0:T(8,128)(2,1)}, bf16[32,1280]{1,0:T(8,128)(2,1)S(1)}, u32[]{:S(2)}, u32[]{:S(2)}) %collective-permute-start.22) | collective-permute-done | bytes 81952 | tf_op jit(solution)/shard_map/ppermute | solution.py:746
  69.2 4.1 %collective-permute-done.32.refs_4_ = bf16[32,1280]{1,0:T(8,128)(2,1)S(1)} collective-permute-done((bf16[32,1280]{1,0:T(8,128)(2,1)S(1)}, bf16[32,1280]{1,0:T(8,128)(2,1)S(1)}, u32[]{:S(2)}, u32[]{:S(2)}) %collective-permute-start.32) | collective-permute-done | bytes 81952 | tf_op jit(solution)/shard_map/ppermute | solution.py:746
  76.5 3.3 %collective-permute-start.24 = (bf16[32,1280]{1,0:T(8,128)(2,1)S(1)}, bf16[32,1280]{1,0:T(8,128)(2,1)S(1)}, u32[]{:S(2)}, u32[]{:S(2)}) collective-permute-start(bf16[32,1280]{1,0:T(8,128)(2,1)S(1)} %get-tuple-element.151), channel_id=1, source_target_pairs={{0,4},{4,0},{8,12},{12,8},{1,5},{5,1},{9,13},{13,9},{2,6},{6,2},{1... | collective-permute-start | bytes 245768 | tf_op jit(solution)/shard_map/ppermute | solution.py:746
  79.9 2.3 %collective-permute-start.26 = (bf16[32,1280]{1,0:T(8,128)(2,1)S(1)}, bf16[32,1280]{1,0:T(8,128)(2,1)S(1)}, u32[]{:S(2)}, u32[]{:S(2)}) collective-permute-start(bf16[32,1280]{1,0:T(8,128)(2,1)S(1)} %get-tuple-element.153), channel_id=1, source_target_pairs={{0,12},{4,8},{8,4},{12,0},{1,13},{5,9},{9,5},{13,1},{2,14},{6,10},... | collective-permute-start | bytes 245768 | tf_op jit(solution)/shard_map/ppermute | solution.py:746
  82.2 2.4 %copy-done.2 = bf16[1280,2000]{0,1:T(8,128)(2,1)S(1)} copy-done((bf16[1280,2000]{0,1:T(8,128)(2,1)S(1)}, bf16[1280,2000]{0,1:T(8,128)(2,1)}, u32[]{:S(2)}) %copy-start.2) | copy-done | bytes 5120024
  86.5 3.4 %collective-permute-done.25.refs_4_ = bf16[32,1280]{1,0:T(8,128)(2,1)S(1)} collective-permute-done((bf16[32,1280]{1,0:T(8,128)(2,1)S(1)}, bf16[32,1280]{1,0:T(8,128)(2,1)S(1)}, u32[]{:S(2)}, u32[]{:S(2)}) %collective-permute-start.25) | collective-permute-done | bytes 81952 | tf_op jit(solution)/shard_map/ppermute | solution.py:746
  91.5 4.5 %collective-permute-start.27 = (bf16[96,1280]{1,0:T(8,128)(2,1)S(1)}, bf16[96,1280]{1,0:T(8,128)(2,1)S(1)}, u32[]{:S(2)}, u32[]{:S(2)}) collective-permute-start(bf16[96,1280]{1,0:T(8,128)(2,1)S(1)} %shard_map.141.refs_0_), channel_id=1, source_target_pairs={{0,4},{4,0},{8,12},{12,8},{1,5},{5,1},{9,13},{13,9},{2,6},{6,2},{1... | collective-permute-start | bytes 737288 | tf_op jit(solution)/shard_map/ppermute | solution.py:746
  99.2 2.6 %collective-permute-done.27.refs_1_ = bf16[96,1280]{1,0:T(8,128)(2,1)S(1)} collective-permute-done((bf16[96,1280]{1,0:T(8,128)(2,1)S(1)}, bf16[96,1280]{1,0:T(8,128)(2,1)S(1)}, u32[]{:S(2)}, u32[]{:S(2)}) %collective-permute-start.27) | collective-permute-done | bytes 245792 | tf_op jit(solution)/shard_map/ppermute | solution.py:746
  103.8 3.6 %collective-permute-done.36.refs_3_ = bf16[96,1280]{1,0:T(8,128)(2,1)S(1)} collective-permute-done((bf16[96,1280]{1,0:T(8,128)(2,1)S(1)}, bf16[96,1280]{1,0:T(8,128)(2,1)S(1)}, u32[]{:S(2)}, u32[]{:S(2)}) %collective-permute-start.36) | collective-permute-done | bytes 245792 | tf_op jit(solution)/shard_map/ppermute | solution.py:1067
  107.4 5.3 %collective-permute-done.38.refs_5_ = bf16[96,1280]{1,0:T(8,128)(2,1)S(1)} collective-permute-done((bf16[96,1280]{1,0:T(8,128)(2,1)S(1)}, bf16[96,1280]{1,0:T(8,128)(2,1)S(1)}, u32[]{:S(2)}, u32[]{:S(2)}) %collective-permute-start.38) | collective-permute-done | bytes 245792 | tf_op jit(solution)/shard_map/ppermute | solution.py:1070
  112.7 3.2 %shard_map.143 = (f32[2048,384]{1,0:T(8,128)S(1)}, bf16[384,1280]{1,0:T(8,128)(2,1)S(1)}, f32[4,16,96]{2,1,0:T(8,128)S(1)}) custom-call(s32[1]{0:T(128)} %bitcast.28.member_ref, bf16[2000,1280]{1,0:T(8,128)(2,1)S(1)} %bitcast.58, bf16[256,1280]{1,0:T(8,128)(2,1)S(1)} %get-tuple-element.121.label_ref, bf16[96,1280]{1,0:T(8,128)(2,1)S(1)} %shard_map.142.refs_0_, ...), custom_call_target="tpu_custom_call" | custom-call | flops 2013265920 | tf_op jit(solution)/shard_map/pallas_call | solution.py:441
  117.2 6.8 %collective-permute-done.39.refs_5_ = bf16[96,1280]{1,0:T(8,128)(2,1)S(1)} collective-permute-done((bf16[96,1280]{1,0:T(8,128)(2,1)S(1)}, bf16[96,1280]{1,0:T(8,128)(2,1)S(1)}, u32[]{:S(2)}, u32[]{:S(2)}) %collective-permute-start.39) | collective-permute-done | bytes 245792 | tf_op jit(solution)/shard_map/ppermute | solution.py:1070
  124.0 3.2 %shard_map.144 = (f32[2048,384]{1,0:T(8,128)S(1)}, bf16[384,1280]{1,0:T(8,128)(2,1)S(1)}, f32[8,16,96]{2,1,0:T(8,128)S(1)}) custom-call(s32[1]{0:T(128)} %bitcast.28.member_ref, bf16[2000,1280]{1,0:T(8,128)(2,1)S(1)} %bitcast.59, bf16[256,1280]{1,0:T(8,128)(2,1)S(1)} %get-tuple-element.121.label_ref, bf16[96,1280]{1,0:T(8,128)(2,1)S(1)} %shard_map.141.refs_0_, ...), custom_call_target="tpu_custom_call" | custom-call | flops 2013265920 | tf_op jit(solution)/shard_map/pallas_call | solution.py:441
  128.7 2.8 %collective-permute-done.40.refs_1_ = f32[8,16,96]{2,1,0:T(8,128)S(1)} collective-permute-done((f32[8,16,96]{2,1,0:T(8,128)S(1)}, f32[8,16,96]{2,1,0:T(8,128)S(1)}, u32[]{:S(2)}, u32[]{:S(2)}) %collective-permute-start.40) | collective-permute-done | bytes 49184 | tf_op jit(solution)/shard_map/ppermute | solution.py:746
  132.5 4.3 %collective-permute-done.42.refs_3_ = f32[8,16,96]{2,1,0:T(8,128)S(1)} collective-permute-done((f32[8,16,96]{2,1,0:T(8,128)S(1)}, f32[8,16,96]{2,1,0:T(8,128)S(1)}, u32[]{:S(2)}, u32[]{:S(2)}) %collective-permute-start.42) | collective-permute-done | bytes 49184 | tf_op jit(solution)/shard_map/ppermute | solution.py:746
  136.8 6.9 %shard_map.145 = (f32[16,768]{1,0:T(8,128)S(1)}, bf16[256,768]{1,0:T(8,128)(2,1)S(1)}, bf16[256,768]{1,0:T(8,128)(2,1)S(1)}, f32[1,4]{1,0:T(1,128)}) custom-call(s32[32]{0:T(128)S(1)} %copy-done.19, s32[16,128]{1,0:T(8,128)S(1)} %get-tuple-element.120.notes_ref, f32[8,16,96]{2,1,0:T(8,128)S(1)} %get-tuple-element.164.refs_0_, ...), custom_call_target="tpu_custom_call" | custom-call | flops 67108864 | tf_op jit(solution)/shard_map/pallas_call | solution.py:632
  143.7 4.9 %shard_map.146 = (bf16[512,1280]{1,0:T(8,128)(2,1)S(1)}, bf16[512,1280]{1,0:T(8,128)(2,1)S(1)}) custom-call(s32[4]{0:T(128)S(1)} %copy-done.20, f32[2048,384]{1,0:T(8,128)S(1)} %get-tuple-element.171.refs_0_, f32[2048,384]{1,0:T(8,128)S(1)} %get-tuple-element.172.refs_1_, bf16[384,1280]{1,0:T(8,128)(2,1)S(1)} %get-tuple-element.173.refs_2_, ...), custom_call_target="tpu_custom_call" | custom-call | flops 2818572288 | tf_op jit(solution)/shard_map/pallas_call | solution.py:683
  149.2 2.8 %shard_map.147.own_ref = bf16[512,1280]{1,0:T(8,128)(2,1)S(1)} custom-call(s32[2]{0:T(128)S(1)} %get-tuple-element.180.order_ref, f32[2048,384]{1,0:T(8,128)S(1)} %get-tuple-element.171.refs_0_, f32[2048,384]{1,0:T(8,128)S(1)} %get-tuple-element.172.refs_1_, bf16[384,1280]{1,0:T(8,128)(2,1)S(1)} %get-tuple-element.173.refs_2_, ...), custom_call_target="tpu_custom_call" | custom-call | flops 1409286144 | tf_op jit(solution)/shard_map/pallas_call | solution.py:683
  154.6 2.0 collective-permute-start.45
  157.0 2.8 %shard_map.149.own_ref = bf16[512,1280]{1,0:T(8,128)(2,1)S(1)} custom-call(s32[2]{0:T(128)S(1)} %get-tuple-element.182.order_ref, f32[2048,384]{1,0:T(8,128)S(1)} %get-tuple-element.171.refs_0_, f32[2048,384]{1,0:T(8,128)S(1)} %get-tuple-element.172.refs_1_, bf16[384,1280]{1,0:T(8,128)(2,1)S(1)} %get-tuple-element.173.refs_2_, ...), custom_call_target="tpu_custom_call" | custom-call | flops 1409286144 | tf_op jit(solution)/shard_map/pallas_call | solution.py:683
  159.9 3.7 %collective-permute-done.46.refs_0_ = bf16[128,1280]{1,0:T(8,128)(2,1)S(1)} collective-permute-done((bf16[128,1280]{1,0:T(8,128)(2,1)S(1)}, bf16[128,1280]{1,0:T(8,128)(2,1)S(1)}, u32[]{:S(2)}, u32[]{:S(2)}) %collective-permute-start.46) | collective-permute-done | bytes 327712 | tf_op jit(solution)/shard_map/ppermute | solution.py:741
  166.0 2.0 collective-permute-start.50
  168.0 2.6 %collective-permute-done.45.refs_0_ = bf16[128,1280]{1,0:T(8,128)(2,1)S(1)} collective-permute-done((bf16[128,1280]{1,0:T(8,128)(2,1)S(1)}, bf16[128,1280]{1,0:T(8,128)(2,1)S(1)}, u32[]{:S(2)}, u32[]{:S(2)}) %collective-permute-start.45) | collective-permute-done | bytes 327712 | tf_op jit(solution)/shard_map/ppermute | solution.py:741
  170.6 6.1 %collective-permute-done.48.refs_1_ = bf16[128,1280]{1,0:T(8,128)(2,1)S(1)} collective-permute-done((bf16[128,1280]{1,0:T(8,128)(2,1)S(1)}, bf16[128,1280]{1,0:T(8,128)(2,1)S(1)}, u32[]{:S(2)}, u32[]{:S(2)}) %collective-permute-start.48) | collective-permute-done | bytes 327712 | tf_op jit(solution)/shard_map/ppermute | solution.py:741
  181.8 6.6 %collective-permute-done.51.refs_2_ = bf16[128,1280]{1,0:T(8,128)(2,1)S(1)} collective-permute-done((bf16[128,1280]{1,0:T(8,128)(2,1)S(1)}, bf16[128,1280]{1,0:T(8,128)(2,1)S(1)}, u32[]{:S(2)}, u32[]{:S(2)}) %collective-permute-start.51) | collective-permute-done | bytes 327712 | tf_op jit(solution)/shard_map/ppermute | solution.py:741
  191.6 3.8 %collective-permute-done.57.refs_3_ = bf16[128,1280]{1,0:T(8,128)(2,1)S(1)} collective-permute-done((bf16[128,1280]{1,0:T(8,128)(2,1)S(1)}, bf16[128,1280]{1,0:T(8,128)(2,1)S(1)}, u32[]{:S(2)}, u32[]{:S(2)}) %collective-permute-start.57) | collective-permute-done | bytes 327712 | tf_op jit(solution)/shard_map/ppermute | solution.py:741
  196.9 4.9 %collective-permute-done.52.refs_0_ = bf16[128,1280]{1,0:T(8,128)(2,1)S(1)} collective-permute-done((bf16[128,1280]{1,0:T(8,128)(2,1)S(1)}, bf16[128,1280]{1,0:T(8,128)(2,1)S(1)}, u32[]{:S(2)}, u32[]{:S(2)}) %collective-permute-start.52) | collective-permute-done | bytes 327712 | tf_op jit(solution)/shard_map/ppermute | solution.py:741
  204.4 2.6 %shard_map.152.refs_4_ = bf16[2000,1280]{1,0:T(8,128)(2,1)} custom-call(s32[12]{0:T(128)S(1)} %stack.122.offsets_ref, bf16[128,1280]{1,0:T(8,128)(2,1)S(1)} %get-tuple-element.189.refs_0_, bf16[128,1280]{1,0:T(8,128)(2,1)S(1)} %get-tuple-element.190.refs_1_, bf16[128,1280]{1,0:T(8,128)(2,1)S(1)} %collective-permute-done.51.refs_2_, ...), custom_call_target="tpu_custom_call" | custom-call | tf_op jit(solution)/shard_map/pallas_call | solution.py:730
  (198 shorter events, 88.1 us)
Async XLA Ops:
  7.4 20.1 %collective-permute-start.8 = (bf16[1280,128]{1,0:T(8,128)(2,1)S(1)}, bf16[1280,128]{1,0:T(8,128)(2,1)S(1)}, u32[]{:S(2)}, u32[]{:S(2)}) collective-permute-start(bf16[1280,128]{1,0:T(8,128)(2,1)S(1)} %get-tuple-element.108), channel_id=1, source_target_pairs={{0,16},{16,0},{1,17},{17,1},{2,18},{18,2},{3,19},{19,3},{4,20},{20... | collective-permute-start | bytes 983048 | tf_op jit(solution)/shard_map/ppermute | solution.py:741
  9.2 18.3 %collective-permute-start.9 = (bf16[128,1280]{1,0:T(8,128)(2,1)S(1)}, bf16[128,1280]{1,0:T(8,128)(2,1)S(1)}, u32[]{:S(2)}, u32[]{:S(2)}) collective-permute-start(bf16[128,1280]{1,0:T(8,128)(2,1)S(1)} %get-tuple-element.109), channel_id=1, source_target_pairs={{0,16},{16,0},{1,17},{17,1},{2,18},{18,2},{3,19},{19,3},{4,20},{20... | collective-permute-start | bytes 983048 | tf_op jit(solution)/shard_map/ppermute | solution.py:741
  36.6 14.7 %collective-permute-start.15 = (bf16[32,1280]{1,0:T(8,128)(2,1)S(1)}, bf16[32,1280]{1,0:T(8,128)(2,1)S(1)}, u32[]{:S(2)}, u32[]{:S(2)}) collective-permute-start(bf16[32,1280]{1,0:T(8,128)(2,1)S(1)} %get-tuple-element.129), channel_id=1, source_target_pairs={{0,4},{4,0},{8,12},{12,8},{1,5},{5,1},{9,13},{13,9},{2,6},{6,2},{1... | collective-permute-start | bytes 245768 | tf_op jit(solution)/shard_map/ppermute | solution.py:746
  37.2 15.7 %collective-permute-start.16 = (bf16[32,1280]{1,0:T(8,128)(2,1)S(1)}, bf16[32,1280]{1,0:T(8,128)(2,1)S(1)}, u32[]{:S(2)}, u32[]{:S(2)}) collective-permute-start(bf16[32,1280]{1,0:T(8,128)(2,1)S(1)} %get-tuple-element.130), channel_id=1, source_target_pairs={{0,8},{4,12},{8,0},{12,4},{1,9},{5,13},{9,1},{13,5},{2,10},{6,14},... | collective-permute-start | bytes 245768 | tf_op jit(solution)/shard_map/ppermute | solution.py:746
  39.6 13.3 %collective-permute-start.17 = (bf16[32,1280]{1,0:T(8,128)(2,1)S(1)}, bf16[32,1280]{1,0:T(8,128)(2,1)S(1)}, u32[]{:S(2)}, u32[]{:S(2)}) collective-permute-start(bf16[32,1280]{1,0:T(8,128)(2,1)S(1)} %get-tuple-element.131), channel_id=1, source_target_pairs={{0,12},{4,8},{8,4},{12,0},{1,13},{5,9},{9,5},{13,1},{2,14},{6,10},... | collective-permute-start | bytes 245768 | tf_op jit(solution)/shard_map/ppermute | solution.py:746
  45.0 14.2 %collective-permute-start.18 = (bf16[32,1280]{1,0:T(8,128)(2,1)}, bf16[32,1280]{1,0:T(8,128)(2,1)S(1)}, u32[]{:S(2)}, u32[]{:S(2)}) collective-permute-start(bf16[32,1280]{1,0:T(8,128)(2,1)} %get-tuple-element.137), channel_id=1, source_target_pairs={{0,4},{4,0},{8,12},{12,8},{1,5},{5,1},{9,13},{13,9},{2,6},{6,2},{1... | collective-permute-start | bytes 245768 | tf_op jit(solution)/shard_map/ppermute | solution.py:746
  50.5 10.3 %collective-permute-start.19 = (bf16[32,1280]{1,0:T(8,128)(2,1)}, bf16[32,1280]{1,0:T(8,128)(2,1)S(1)}, u32[]{:S(2)}, u32[]{:S(2)}) collective-permute-start(bf16[32,1280]{1,0:T(8,128)(2,1)} %get-tuple-element.138), channel_id=1, source_target_pairs={{0,8},{4,12},{8,0},{12,4},{1,9},{5,13},{9,1},{13,5},{2,10},{6,14},... | collective-permute-start | bytes 245768 | tf_op jit(solution)/shard_map/ppermute | solution.py:746
  57.5 10.8 %collective-permute-start.22 = (bf16[32,1280]{1,0:T(8,128)(2,1)}, bf16[32,1280]{1,0:T(8,128)(2,1)S(1)}, u32[]{:S(2)}, u32[]{:S(2)}) collective-permute-start(bf16[32,1280]{1,0:T(8,128)(2,1)} %copy-done.23), channel_id=1, source_target_pairs={{0,8},{4,12},{8,0},{12,4},{1,9},{5,13},{9,1},{13,5},{2,10},{6,14},... | collective-permute-start | bytes 245768 | tf_op jit(solution)/shard_map/ppermute | solution.py:746
  63.2 10.1 %collective-permute-start.32 = (bf16[32,1280]{1,0:T(8,128)(2,1)S(1)}, bf16[32,1280]{1,0:T(8,128)(2,1)S(1)}, u32[]{:S(2)}, u32[]{:S(2)}) collective-permute-start(bf16[32,1280]{1,0:T(8,128)(2,1)S(1)} %get-tuple-element.158), channel_id=1, source_target_pairs={{0,8},{4,12},{8,0},{12,4},{1,9},{5,13},{9,1},{13,5},{2,10},{6,14},... | collective-permute-start | bytes 245768 | tf_op jit(solution)/shard_map/ppermute | solution.py:746
  74.1 16.7 %collective-permute-start.34 = (bf16[96,1280]{1,0:T(8,128)(2,1)S(1)}, bf16[96,1280]{1,0:T(8,128)(2,1)S(1)}, u32[]{:S(2)}, u32[]{:S(2)}) collective-permute-start(bf16[96,1280]{1,0:T(8,128)(2,1)S(1)} %shard_map.142.refs_0_), channel_id=1, source_target_pairs={{0,4},{4,0},{8,12},{12,8},{1,5},{5,1},{9,13},{13,9},{2,6},{6,2},{1... | collective-permute-start | bytes 737288 | tf_op jit(solution)/shard_map/ppermute | solution.py:746
  75.6 15.2 %collective-permute-start.35 = (bf16[96,1280]{1,0:T(8,128)(2,1)S(1)}, bf16[96,1280]{1,0:T(8,128)(2,1)S(1)}, u32[]{:S(2)}, u32[]{:S(2)}) collective-permute-start(bf16[96,1280]{1,0:T(8,128)(2,1)S(1)} %shard_map.142.refs_0_), channel_id=1, source_target_pairs={{4,8},{8,4},{5,9},{9,5},{6,10},{10,6},{7,11},{11,7},{20,24},{24,20... | collective-permute-start | bytes 737288 | tf_op jit(solution)/shard_map/ppermute | solution.py:1064
  76.5 10.1 %collective-permute-start.24 = (bf16[32,1280]{1,0:T(8,128)(2,1)S(1)}, bf16[32,1280]{1,0:T(8,128)(2,1)S(1)}, u32[]{:S(2)}, u32[]{:S(2)}) collective-permute-start(bf16[32,1280]{1,0:T(8,128)(2,1)S(1)} %get-tuple-element.151), channel_id=1, source_target_pairs={{0,4},{4,0},{8,12},{12,8},{1,5},{5,1},{9,13},{13,9},{2,6},{6,2},{1... | collective-permute-start | bytes 245768 | tf_op jit(solution)/shard_map/ppermute | solution.py:746
  79.7 10.2 %collective-permute-start.25 = (bf16[32,1280]{1,0:T(8,128)(2,1)S(1)}, bf16[32,1280]{1,0:T(8,128)(2,1)S(1)}, u32[]{:S(2)}, u32[]{:S(2)}) collective-permute-start(bf16[32,1280]{1,0:T(8,128)(2,1)S(1)} %get-tuple-element.152), channel_id=1, source_target_pairs={{0,8},{4,12},{8,0},{12,4},{1,9},{5,13},{9,1},{13,5},{2,10},{6,14},... | collective-permute-start | bytes 245768 | tf_op jit(solution)/shard_map/ppermute | solution.py:746
  91.5 10.4 %collective-permute-start.27 = (bf16[96,1280]{1,0:T(8,128)(2,1)S(1)}, bf16[96,1280]{1,0:T(8,128)(2,1)S(1)}, u32[]{:S(2)}, u32[]{:S(2)}) collective-permute-start(bf16[96,1280]{1,0:T(8,128)(2,1)S(1)} %shard_map.141.refs_0_), channel_id=1, source_target_pairs={{0,4},{4,0},{8,12},{12,8},{1,5},{5,1},{9,13},{13,9},{2,6},{6,2},{1... | collective-permute-start | bytes 737288 | tf_op jit(solution)/shard_map/ppermute | solution.py:746
  96.6 10.8 %collective-permute-start.36 = (bf16[96,1280]{1,0:T(8,128)(2,1)S(1)}, bf16[96,1280]{1,0:T(8,128)(2,1)S(1)}, u32[]{:S(2)}, u32[]{:S(2)}) collective-permute-start(bf16[96,1280]{1,0:T(8,128)(2,1)S(1)} %collective-permute-done.35.refs_2_), channel_id=1, source_target_pairs={{4,0},{8,12},{5,1},{9,13},{6,2},{10,14},{7,3},{11,15},{20,16},{24,... | collective-permute-start | bytes 737288 | tf_op jit(solution)/shard_map/ppermute | solution.py:1067
  97.9 14.7 %collective-permute-start.38 = (bf16[96,1280]{1,0:T(8,128)(2,1)S(1)}, bf16[96,1280]{1,0:T(8,128)(2,1)S(1)}, u32[]{:S(2)}, u32[]{:S(2)}) collective-permute-start(bf16[96,1280]{1,0:T(8,128)(2,1)S(1)} %collective-permute-done.37.refs_4_), channel_id=1, source_target_pairs={{4,0},{8,12},{5,1},{9,13},{6,2},{10,14},{7,3},{11,15},{20,16},{24,... | collective-permute-start | bytes 737288 | tf_op jit(solution)/shard_map/ppermute | solution.py:1070
  101.9 14.0 %collective-permute-start.30 = (bf16[96,1280]{1,0:T(8,128)(2,1)S(1)}, bf16[96,1280]{1,0:T(8,128)(2,1)S(1)}, u32[]{:S(2)}, u32[]{:S(2)}) collective-permute-start(bf16[96,1280]{1,0:T(8,128)(2,1)S(1)} %collective-permute-done.27.refs_1_), channel_id=1, source_target_pairs={{4,8},{8,4},{5,9},{9,5},{6,10},{10,6},{7,11},{11,7},{20,24},{24,20... | collective-permute-start | bytes 737288 | tf_op jit(solution)/shard_map/ppermute | solution.py:1066
  102.5 14.7 %collective-permute-start.29 = (bf16[96,1280]{1,0:T(8,128)(2,1)S(1)}, bf16[96,1280]{1,0:T(8,128)(2,1)S(1)}, u32[]{:S(2)}, u32[]{:S(2)}) collective-permute-start(bf16[96,1280]{1,0:T(8,128)(2,1)S(1)} %collective-permute-done.28.refs_2_), channel_id=1, source_target_pairs={{4,0},{8,12},{5,1},{9,13},{6,2},{10,14},{7,3},{11,15},{20,16},{24,... | collective-permute-start | bytes 737288 | tf_op jit(solution)/shard_map/ppermute | solution.py:1067
  148.7 11.1 %collective-permute-start.44 = (bf16[512,1280]{1,0:T(8,128)(2,1)S(1)}, bf16[512,1280]{1,0:T(8,128)(2,1)S(1)}, u32[]{:S(2)}, u32[]{:S(2)}) collective-permute-start(bf16[512,1280]{1,0:T(8,128)(2,1)S(1)} %get-tuple-element.183), channel_id=1, source_target_pairs={{0,1},{1,0},{2,3},{3,2},{4,5},{5,4},{6,7},{7,6},{8,9},{9,8},{10,11... | collective-permute-start | bytes 3932168 | tf_op jit(solution)/shard_map/ppermute | solution.py:741
  152.9 10.6 %collective-permute-start.46 = (bf16[128,1280]{1,0:T(8,128)(2,1)S(1)}, bf16[128,1280]{1,0:T(8,128)(2,1)S(1)}, u32[]{:S(2)}, u32[]{:S(2)}) collective-permute-start(bf16[128,1280]{1,0:T(8,128)(2,1)S(1)} %get-tuple-element.181), channel_id=1, source_target_pairs={{0,16},{16,0},{1,17},{17,1},{2,18},{18,2},{3,19},{19,3},{4,20},{20... | collective-permute-start | bytes 983048 | tf_op jit(solution)/shard_map/ppermute | solution.py:741
  153.0 10.6 %collective-permute-start.47 = (bf16[128,1280]{1,0:T(8,128)(2,1)S(1)}, bf16[128,1280]{1,0:T(8,128)(2,1)S(1)}, u32[]{:S(2)}, u32[]{:S(2)}) collective-permute-start(bf16[128,1280]{1,0:T(8,128)(2,1)S(1)} %get-tuple-element.185), channel_id=1, source_target_pairs={{0,2},{2,0},{1,3},{3,1},{4,6},{6,4},{5,7},{7,5},{8,10},{10,8},{9,1... | collective-permute-start | bytes 983048 | tf_op jit(solution)/shard_map/ppermute | solution.py:741
  154.6 16.0 %collective-permute-start.45 = (bf16[128,1280]{1,0:T(8,128)(2,1)S(1)}, bf16[128,1280]{1,0:T(8,128)(2,1)S(1)}, u32[]{:S(2)}, u32[]{:S(2)}) collective-permute-start(bf16[128,1280]{1,0:T(8,128)(2,1)S(1)} %get-tuple-element.184), channel_id=1, source_target_pairs={{0,16},{16,0},{1,17},{17,1},{2,18},{18,2},{3,19},{19,3},{4,20},{20... | collective-permute-start | bytes 983048 | tf_op jit(solution)/shard_map/ppermute | solution.py:741
  156.5 14.1 %collective-permute-start.49 = (bf16[128,1280]{1,0:T(8,128)(2,1)S(1)}, bf16[128,1280]{1,0:T(8,128)(2,1)S(1)}, u32[]{:S(2)}, u32[]{:S(2)}) collective-permute-start(bf16[128,1280]{1,0:T(8,128)(2,1)S(1)} %get-tuple-element.187), channel_id=1, source_target_pairs={{0,2},{2,0},{1,3},{3,1},{4,6},{6,4},{5,7},{7,5},{8,10},{10,8},{9,1... | collective-permute-start | bytes 983048 | tf_op jit(solution)/shard_map/ppermute | solution.py:741
  164.4 12.4 %collective-permute-start.48 = (bf16[128,1280]{1,0:T(8,128)(2,1)S(1)}, bf16[128,1280]{1,0:T(8,128)(2,1)S(1)}, u32[]{:S(2)}, u32[]{:S(2)}) collective-permute-start(bf16[128,1280]{1,0:T(8,128)(2,1)S(1)} %get-tuple-element.186), channel_id=1, source_target_pairs={{0,2},{2,0},{1,3},{3,1},{4,6},{6,4},{5,7},{7,5},{8,10},{10,8},{9,1... | collective-permute-start | bytes 983048 | tf_op jit(solution)/shard_map/ppermute | solution.py:741
  166.0 10.8 %collective-permute-start.50 = (bf16[128,1280]{1,0:T(8,128)(2,1)S(1)}, bf16[128,1280]{1,0:T(8,128)(2,1)S(1)}, u32[]{:S(2)}, u32[]{:S(2)}) collective-permute-start(bf16[128,1280]{1,0:T(8,128)(2,1)S(1)} %get-tuple-element.188), channel_id=1, source_target_pairs={{0,16},{16,0},{1,17},{17,1},{2,18},{18,2},{3,19},{19,3},{4,20},{20... | collective-permute-start | bytes 983048 | tf_op jit(solution)/shard_map/ppermute | solution.py:741
  177.6 10.7 %collective-permute-start.51 = (bf16[128,1280]{1,0:T(8,128)(2,1)S(1)}, bf16[128,1280]{1,0:T(8,128)(2,1)S(1)}, u32[]{:S(2)}, u32[]{:S(2)}) collective-permute-start(bf16[128,1280]{1,0:T(8,128)(2,1)S(1)} %get-tuple-element.189.refs_0_), channel_id=1, source_target_pairs={{0,2},{2,0},{1,3},{3,1},{4,6},{6,4},{5,7},{7,5},{8,10},{10,8},{9,1... | collective-permute-start | bytes 983048 | tf_op jit(solution)/shard_map/ppermute | solution.py:741
  179.2 10.8 %collective-permute-start.53 = (bf16[128,1280]{1,0:T(8,128)(2,1)S(1)}, bf16[128,1280]{1,0:T(8,128)(2,1)S(1)}, u32[]{:S(2)}, u32[]{:S(2)}) collective-permute-start(bf16[128,1280]{1,0:T(8,128)(2,1)S(1)} %get-tuple-element.190.refs_1_), channel_id=1, source_target_pairs={{0,16},{16,0},{1,17},{17,1},{2,18},{18,2},{3,19},{19,3},{4,20},{20... | collective-permute-start | bytes 983048 | tf_op jit(solution)/shard_map/ppermute | solution.py:741
  180.9 14.5 %collective-permute-start.57 = (bf16[128,1280]{1,0:T(8,128)(2,1)S(1)}, bf16[128,1280]{1,0:T(8,128)(2,1)S(1)}, u32[]{:S(2)}, u32[]{:S(2)}) collective-permute-start(bf16[128,1280]{1,0:T(8,128)(2,1)S(1)} %get-tuple-element.190.refs_1_), channel_id=1, source_target_pairs={{0,2},{2,0},{1,3},{3,1},{4,6},{6,4},{5,7},{7,5},{8,10},{10,8},{9,1... | collective-permute-start | bytes 983048 | tf_op jit(solution)/shard_map/ppermute | solution.py:741
  181.4 15.5 %collective-permute-start.58 = (bf16[128,1280]{1,0:T(8,128)(2,1)S(1)}, bf16[128,1280]{1,0:T(8,128)(2,1)S(1)}, u32[]{:S(2)}, u32[]{:S(2)}) collective-permute-start(bf16[128,1280]{1,0:T(8,128)(2,1)S(1)} %get-tuple-element.189.refs_0_), channel_id=1, source_target_pairs={{0,16},{16,0},{1,17},{17,1},{2,18},{18,2},{3,19},{19,3},{4,20},{20... | collective-permute-start | bytes 983048 | tf_op jit(solution)/shard_map/ppermute | solution.py:741
  188.4 13.5 %collective-permute-start.52 = (bf16[128,1280]{1,0:T(8,128)(2,1)S(1)}, bf16[128,1280]{1,0:T(8,128)(2,1)S(1)}, u32[]{:S(2)}, u32[]{:S(2)}) collective-permute-start(bf16[128,1280]{1,0:T(8,128)(2,1)S(1)} %collective-permute-done.51.refs_2_), channel_id=1, source_target_pairs={{0,16},{16,0},{1,17},{17,1},{2,18},{18,2},{3,19},{19,3},{4,20},{20... | collective-permute-start | bytes 983048 | tf_op jit(solution)/shard_map/ppermute | solution.py:741
  190.0 11.8 %collective-permute-start.54 = (bf16[128,1280]{1,0:T(8,128)(2,1)S(1)}, bf16[128,1280]{1,0:T(8,128)(2,1)S(1)}, u32[]{:S(2)}, u32[]{:S(2)}) collective-permute-start(bf16[128,1280]{1,0:T(8,128)(2,1)S(1)} %collective-permute-done.53.refs_5_), channel_id=1, source_target_pairs={{0,2},{2,0},{1,3},{3,1},{4,6},{6,4},{5,7},{7,5},{8,10},{10,8},{9,1... | collective-permute-start | bytes 983048 | tf_op jit(solution)/shard_map/ppermute | solution.py:741
  191.6 10.8 %collective-permute-start.59 = (bf16[128,1280]{1,0:T(8,128)(2,1)S(1)}, bf16[128,1280]{1,0:T(8,128)(2,1)S(1)}, u32[]{:S(2)}, u32[]{:S(2)}) collective-permute-start(bf16[128,1280]{1,0:T(8,128)(2,1)S(1)} %get-tuple-element.189.refs_0_), channel_id=1, source_target_pairs={{0,1},{1,0},{2,3},{3,2},{4,5},{5,4},{6,7},{7,6},{8,9},{9,8},{10,11... | collective-permute-start | bytes 983048 | tf_op jit(solution)/shard_map/ppermute | solution.py:741
  (63 other events, 539.9 us)
